TPU v7x, 256 devices: a whole 4x4x8 slice. The times are simulated.
256 devices in a mesh: lines: 32 (over x, z), slab: 8 (over y, core).
Axes of the slice: x: 4, y: 4, z: 8, core: 2. Of those that a mesh axis runs over, the one named last changes fastest.
Arguments:
- fields: float32 [6, 2097152], P(None, ('lines', 'slab')), may hold values from -6 to 6
- frac_x: float32 [2097152], P(('lines', 'slab')), may hold values from 0 to 1
- owner: int32 [2097152], P(('lines', 'slab')), may hold values from 0 to 31, as said below
- slab: int32 [2097152], P(('lines', 'slab')), may hold values from 0 to 7
- line_in: int32 [2097152], P(('lines', 'slab')), may hold values from 0 to 63
- xcell: int32 [2097152], P(('lines', 'slab')), may hold values from 0 to 511, as said below
- tile_count: int32 [16384], P(('lines', 'slab')), may hold values from 64 to 128, as said below
- y_offset: int32 [512, 64, 256], P('lines', 'slab'), may hold values from -2 to 2
- y_frac: float32 [512, 64, 256], P('lines', 'slab'), may hold values from 0 to 1
Outputs:
- remeshed: float32 [6, 512, 64, 256], P(None, 'lines', 'slab')
Inputs may be any that keep to these rules, and one draw needn't show every extreme that they name: Tile t of a device holds its live particles in the first tile_count[t] of its 128 slots; the other slots are empty and whatever they hold is ignored. The first tile of every device is full. Among the live particles of one device at most 48 share one pair of owner and slab, and in every draw one such pair holds exactly 48 of them. Among the live particles of one device at most 48 share one pair of x range (xcell div 16) and slab, and in every draw one such pair holds exactly 48 of them.
All inputs are finite; a program needn't handle non-finite values.
Results may differ from a plain program's by a relative error of at most 0.00002.
Values sent between devices are 32-bit elements; how exact they have to be, the bound alone decides.
No kernel may reach another device: no remote copies, remote signals or barrier semaphores. Data moves between devices by JAX's collectives and lax.ppermute only.
A program may use at most 128 MiB of HBM per device.

v0:
```python
import jax
import jax.numpy as jnp
from jax import lax
from jax.sharding import PartitionSpec as P


def kernel_weights(offset):
    remain = 1.0 - offset
    return (
        -0.5 * offset * remain * remain,
        1.0 - 2.5 * offset * offset + 1.5 * offset * offset * offset,
        1.0 - 2.5 * remain * remain + 1.5 * remain * remain * remain,
        -0.5 * offset * offset * remain,
    )


def send_particles(payload, location, target, alive_slot, line_count, slab_count, capacity):
    targets = line_count * slab_count
    sort_key = jnp.where(alive_slot, target, targets)
    sort_order = jnp.argsort(sort_key, stable=True)
    sorted_key = sort_key[sort_order]
    starts = jnp.searchsorted(sorted_key, jnp.arange(targets, dtype=jnp.int32))
    within = (
        jnp.arange(sorted_key.shape[0], dtype=jnp.int32)
        - starts[jnp.minimum(sorted_key, targets - 1)]
    )
    slot_index = jnp.where(sorted_key < targets, sorted_key * capacity + within, targets * capacity)
    floats_out = jnp.zeros((payload.shape[0], targets * capacity), jnp.float32)
    floats_out = floats_out.at[:, slot_index].set(payload[:, sort_order], mode="drop")
    cells_out = jnp.zeros((1, targets * capacity), jnp.int32)
    cells_out = cells_out.at[:, slot_index].set(location[sort_order][None, :], mode="drop")
    floats_out = floats_out.reshape(payload.shape[0], line_count, slab_count, capacity)
    cells_out = cells_out.reshape(1, line_count, slab_count, capacity)
    arrived, landing = (
        lax.all_to_all(
            lax.all_to_all(floats_out, "lines", split_axis=1, concat_axis=1, tiled=True),
            "slab",
            split_axis=2,
            concat_axis=2,
            tiled=True,
        ),
        lax.all_to_all(
            lax.all_to_all(cells_out, "lines", split_axis=1, concat_axis=1, tiled=True),
            "slab",
            split_axis=2,
            concat_axis=2,
            tiled=True,
        ),
    )
    return (arrived.reshape(payload.shape[0], -1), landing.reshape(-1))


def deposit(carried, offset, index_list, cells):
    weights = kernel_weights(offset)
    spread = jnp.concatenate([carried * weight[None, :] for weight in weights], axis=1)
    landing_cells = jnp.concatenate(index_list)
    return jnp.zeros((carried.shape[0], cells), jnp.float32).at[:, landing_cells].add(spread)


def y_pass(lattice, y_offset, y_frac):
    weights = kernel_weights(y_frac)
    result = jnp.zeros_like(lattice)
    for travel in range(-3, 5):
        factor = jnp.zeros_like(y_frac)
        for shift_cells in range(-2, 3):
            neighbor = travel - shift_cells
            if -1 <= neighbor <= 2:
                factor = factor + jnp.where(y_offset == shift_cells, weights[neighbor + 1], 0.0)
        result = result + jnp.roll(lattice * factor[None], travel, axis=3)
    return result


def per_device(fields, frac_x, owner, slab, line_in, xcell, tile_count, y_offset, y_frac):
    line_count = lax.axis_size("lines")
    slab_count = lax.axis_size("slab")
    part_count = fields.shape[1]
    field_count = fields.shape[0]
    tile_size = part_count // tile_count.shape[0]
    alive_slot = jnp.arange(part_count, dtype=jnp.int32) % tile_size < jnp.repeat(
        tile_count, tile_size, total_repeat_length=part_count
    )
    x_width = y_offset.shape[0]
    z_planes = y_offset.shape[1]
    y_cells = y_offset.shape[2]
    x_cells = x_width * line_count
    y_lines = y_cells // line_count
    capacity = 3 * part_count // (2 * line_count * slab_count)
    y_inside = line_in // z_planes
    z_inside = line_in % z_planes
    payload = jnp.concatenate([fields, frac_x[None, :]], axis=0)
    location = (z_inside * y_lines + y_inside) * x_cells + xcell
    arrived, landing = send_particles(
        payload, location, owner * slab_count + slab, alive_slot, line_count, slab_count, capacity
    )
    x_inside = landing % x_cells
    row_start = landing - x_inside
    index_list = [row_start + (x_inside + neighbor) % x_cells for neighbor in (-1, 0, 1, 2)]
    deposited = deposit(
        arrived[:field_count], arrived[field_count], index_list, z_planes * y_lines * x_cells
    )
    deposited = deposited.reshape(field_count, z_planes, y_lines, x_cells)
    turned = lax.all_to_all(deposited, "lines", split_axis=3, concat_axis=2, tiled=True)
    lattice = jnp.transpose(turned, (0, 3, 1, 2))
    return y_pass(lattice, y_offset, y_frac)


def solution(mesh):
    return jax.shard_map(
        per_device,
        mesh=mesh,
        in_specs=(
            P(None, ("lines", "slab")),
            P(("lines", "slab")),
            P(("lines", "slab")),
            P(("lines", "slab")),
            P(("lines", "slab")),
            P(("lines", "slab")),
            P(("lines", "slab")),
            P("lines", "slab", None),
            P("lines", "slab", None),
        ),
        out_specs=P(None, "lines", "slab", None),
        check_vma=False,
    )
```

profile of v0, /device:TPU:1, one launch (start us, length us, event | category | flops | bytes accessed | tf_op | source)
XLA Modules:
  0.0 794.5 jit_solution(1026195907454951732)
XLA Ops:
  0.0 2.1 fusion.54
  3.7 2.1 fusion.52
  5.8 2.1 fusion.53
  7.9 4.4 compare_select_fusion.4
  12.3 5.8 compare_reduce_fusion.56
  18.1 36.7 %add_select_fusion.8 = s32[8192]{0:T(1024)S(1)} fusion(s32[8192]{0:T(1024)} %param.16, s32[8192]{0:T(1024)} %param.15, pred[8192]{0:T(1024)(128)(4,1)S(1)} %get-tuple-element.158, pred[8192]{0:T(1024)(128)(4,1)S(1)} %get-tuple-element.157, pred[8192]{0:T(1024)(128)(4,1)S(1)} %get-tuple-element.156, pred[8192]{0:T(1024)(128)(4,1)S(1)} %get-tuple-element.155, ...), kind=kLoop, calls=%fused_computation.187 | loop fusion | flops 622592 | bytes 598244 | tf_op jit(solution)/shard_map/jit(_where)/select_n | solution.py:19
  54.8 6.8 sort.17
  62.4 46.0 %gather_fusion.1 = s32[8192]{0:T(1024)S(1)} fusion(s32[8192]{0:T(1024)S(1)} %add_select_fusion.8, s32[8192]{0:T(1024)S(1)} %get-tuple-element.275), kind=kCustom, calls=%fused_computation.1 | custom fusion | bytes 98304 | tf_op jit(solution)/shard_map/gather | solution.py:21
  108.5 25.1 %while.25 = (s32[]{:T(128)}, u32[256]{0:T(256)S(1)}, u32[256]{0:T(256)S(1)}, s32[8192]{0:T(1024)S(1)}, s32[]{:T(128)}, /*index=5*/s32[]{:T(128)}, s32[]{}) while((s32[]{:T(128)}, u32[256]{0:T(256)S(1)}, u32[256]{0:T(256)S(1)}, s32[8192]{0:T(1024)S(1)}, s32[]{:T(128)}, /*index=5*/s32[]{:T(128)}, s32[]{}) %tuple.186), condition=%wide.region_2.3_spmd.clone, body=%wide.region_1.2_spmd.clone.sunk | while | flops 4356 | bytes 16484 | solution.py:22
  133.6 45.5 %gather_fusion.3 = s32[8192]{0:T(1024)S(1)} fusion(s32[8192]{0:T(1024)S(1)} %get-tuple-element.274, s32[8192]{0:T(1024)S(1)} %get-tuple-element.275), kind=kCustom, calls=%fused_computation.3 | custom fusion | bytes 98304 | tf_op jit(solution)/shard_map/gather | solution.py:31
  179.1 51.0 %gather_fusion.2 = s32[8192]{0:T(1024)S(1)} fusion(s32[256]{0:T(256)S(1)} %convert_element_type.10, s32[8192]{0:T(1024)S(1)} %broadcast_clamp_fusion), kind=kCustom, calls=%fused_computation.2 | custom fusion | bytes 98304 | tf_op jit(solution)/shard_map/gather | solution.py:25
  230.2 30.5 %scatter_custom_fusion = s32[12288]{0:T(1024)S(1)} fusion(s32[8192]{0:T(1024)S(1)} %bitcast.165, s32[8192]{0:T(1024)S(1)} %gather_fusion.3, s32[]{:T(128)} %constant.198.clone.1), kind=kCustom, calls=%fused_computation.197 | custom fusion | bytes 49156 | tf_op jit(solution)/shard_map/scatter | solution.py:31
  260.9 20.5 %all_to_all.38 = s32[32,1,384]{2,1,0:T(1,128)S(1)} all-to-all(s32[32,1,384]{2,1,0:T(1,128)S(1)} %reshape.707), channel_id=1, replica_groups=mesh['lines'=32,'slab'=8] {'lines'}, dimensions={0} | all-to-all | bytes 98304 | tf_op jit(solution)/shard_map/all_to_all | solution.py:43
  283.6 6.6 all-to-all-start.1
  290.2 2.7 copy.126
  293.0 69.6 %scatter_custom_fusion.1 = f32[7,12288]{0,1:T(8,128)} fusion(s32[8192]{0:T(1024)S(1)} %bitcast.166, f32[7,8192]{0,1:T(8,128)} %copy.126, s32[8192]{0:T(1024)S(1)} %get-tuple-element.275, f32[]{:T(128)} %constant.197.clone.1), kind=kCustom, calls=%fused_computation.18 | custom fusion | bytes 344576 | tf_op jit(solution)/shard_map/scatter | solution.py:29
  362.6 4.8 copy.127
  369.0 4.0 all-to-all-start.2
  374.2 11.1 %all-to-all-done.2 = f32[32,1,2688]{2,1,0:T(1,128)S(1)} async-done(((f32[32,1,2688]{2,1,0:T(1,128)}), f32[32,1,2688]{2,1,0:T(1,128)S(1)}, u32[]{:S(2)}, u32[]{:S(2)}) %all-to-all-start.2) | async-done | bytes 344096 | tf_op jit(solution)/shard_map/all_to_all | solution.py:36
  389.4 6.3 all-to-all-start.3
  395.8 7.1 all-to-all-done.3
  406.3 13.1 %copy.131 = f32[49152,6]{1,0:T(8,128)} copy(f32[49152,6]{0,1:T(8,128)S(1)} %maximum_bitcast_fusion) | data formatting | bytes 2359296 | tf_op jit(solution)/shard_map/concatenate | solution.py:55
  419.4 279.2 %scatter_custom_fusion.2 = f32[6,32768]{0,1:T(8,128)} fusion(s32[49152]{0:T(1024)S(1)} %bitcast.152, f32[49152,6]{1,0:T(8,128)} %copy.131, f32[]{:T(128)} %constant.197.clone.1), kind=kCustom, calls=%fused_computation.16 | custom fusion | flops 294912 | bytes 786944 | tf_op jit(solution)/shard_map/scatter-add | solution.py:57
  698.6 30.8 %copy.132 = f32[6,8,8,512]{2,1,0,3:T(8,128)} copy(f32[6,8,8,512]{0,3,2,1:T(8,128)} %bitcast.134) | data formatting | bytes 1572864 | tf_op jit(solution)/shard_map/reshape | solution.py:101
  729.4 10.4 %reshape.715 = f32[32,1,6144]{2,1,0:T(1,128)} reshape(f32[512,6,8,8]{3,2,1,0:T(8,128)} %bitcast.135) | data formatting | bytes 1572864
  739.8 5.4 all-to-all-start.4
  745.7 19.3 %all-to-all-done.4 = f32[32,1,6144]{2,1,0:T(1,128)S(1)} async-done(((f32[32,1,6144]{2,1,0:T(1,128)}), f32[32,1,6144]{2,1,0:T(1,128)S(1)}, u32[]{:S(2)}, u32[]{:S(2)}) %all-to-all-start.4) | async-done | bytes 786464 | tf_op jit(solution)/shard_map/all_to_all | solution.py:102
  765.0 2.4 reduce.120
  767.4 8.5 %reshape.716 = f32[512,6,8,8]{3,2,1,0:T(8,128)} reshape(f32[32,6144]{1,0:T(8,128)S(1)} %reduce.120) | data formatting | bytes 1572864
  775.9 9.8 %copy.134 = f32[6,8,32,8,16]{4,3,2,1,0:T(8,128)} copy(f32[6,8,32,8,16]{3,1,0,4,2:T(8,128)} %bitcast.136) | data formatting | bytes 1572864 | tf_op jit(solution)/shard_map/all_to_all | solution.py:102
  785.8 4.4 copy.135
  792.2 2.1 fusion.14
  (122 shorter events, 42.2 us)
Async XLA Ops:
  179.1 111.0 %copy-start.1 = (f32[6,8192]{1,0:T(8,128)S(1)}, f32[6,8192]{1,0:T(8,128)}, u32[]{:S(2)}) copy-start(f32[6,8192]{1,0:T(8,128)} %param.13) | copy-start | bytes 589828
  179.1 111.0 %copy-start.3 = (f32[8192]{0:T(1024)S(1)}, f32[8192]{0:T(1024)}, u32[]{:S(2)}) copy-start(f32[8192]{0:T(1024)} %param.14) | copy-start | bytes 98308
  283.6 85.4 %all-to-all-start.1 = ((s32[8,1,1536]{2,1,0:T(1,128)}), s32[8,1,1536]{2,1,0:T(1,128)S(1)}, u32[]{:S(2)}, u32[]{:S(2)}) async-start(s32[8,1,1536]{2,1,0:T(1,128)} %reshape.709), calls=%async_computation.1 | async-start | bytes 98304 | tf_op jit(solution)/shard_map/all_to_all | solution.py:42
  369.0 16.3 %all-to-all-start.2 = ((f32[32,1,2688]{2,1,0:T(1,128)}), f32[32,1,2688]{2,1,0:T(1,128)S(1)}, u32[]{:S(2)}, u32[]{:S(2)}) async-start(f32[32,1,2688]{2,1,0:T(1,128)} %reshape.711), calls=%async_computation.2 | async-start | bytes 688128 | tf_op jit(solution)/shard_map/all_to_all | solution.py:36
  389.4 13.5 %all-to-all-start.3 = ((f32[8,1,10752]{2,1,0:T(1,128)}), f32[8,1,10752]{2,1,0:T(1,128)S(1)}, u32[]{:S(2)}, u32[]{:S(2)}) async-start(f32[8,1,10752]{2,1,0:T(1,128)} %reshape.713), calls=%async_computation.3 | async-start | bytes 688128 | tf_op jit(solution)/shard_map/all_to_all | solution.py:35
  729.4 15.8 %copy-start = (f32[16,8,256]{2,1,0:T(8,128)S(1)}, f32[16,8,256]{2,1,0:T(8,128)}, u32[]{:S(2)}) copy-start(f32[16,8,256]{2,1,0:T(8,128)} %param.21) | copy-start | bytes 393220
  729.4 15.8 %copy-start.2 = (s32[16,8,256]{2,1,0:T(8,128)S(1)}, s32[16,8,256]{2,1,0:T(8,128)}, u32[]{:S(2)}) copy-start(s32[16,8,256]{2,1,0:T(8,128)} %param.20) | copy-start | bytes 393220
  739.8 25.2 %all-to-all-start.4 = ((f32[32,1,6144]{2,1,0:T(1,128)}), f32[32,1,6144]{2,1,0:T(1,128)S(1)}, u32[]{:S(2)}, u32[]{:S(2)}) async-start(f32[32,1,6144]{2,1,0:T(1,128)} %reshape.715), calls=%async_computation.4 | async-start | bytes 1572864 | tf_op jit(solution)/shard_map/all_to_all | solution.py:102
where the time goes:
time: 807 us; the launch traced here: 795 us
  local copies, waits for them, and re-layouts  369 us (46%)
  other arithmetic  344 us (43%)
  waiting for transfers between devices  37.5 us (5%)
  starting transfers between devices  22.2 us (3%)
  blocking collectives  20.5 us (3%)
    scatter-add x1, other arithmetic, deposit(): jnp.zeros((carried.shape[0], cells), jnp.float32).at[:, landing_cells]  279 us
    scatter x1, local copies, waits for them, and re-layouts, send_particles(): floats_out.at[:, slot_index].set(payload[:, sort_order], mode='drop')  69.6 us
    gather x1, local copies, waits for them, and re-layouts, send_particles(): starts[jnp.minimum(sorted_key, targets - 1)]  51 us
    gather x1, local copies, waits for them, and re-layouts, send_particles(): sorted_key = sort_key[sort_order]  46 us
    gather x1, local copies, waits for them, and re-layouts, send_particles(): location[sort_order][None, :]  45.5 us
    select_n x1, other arithmetic, send_particles(): sort_key = jnp.where(alive_slot, target, targets)  36.7 us
    reshape x1, local copies, waits for them, and re-layouts, per_device(): deposited = deposited.reshape(field_count, z_planes, y_lines, x_cells)  30.8 us
    scatter x1, local copies, waits for them, and re-layouts, send_particles(): cells_out.at[:, slot_index].set(location[sort_order][None, :], mode='drop')  30.5 us
  transfers between devices with their start and end apart: 4, of which 3 were waited for; matrix products, arithmetic and copies ran while one was open for 10% of the time, Pallas kernels for 0%

commit v1 on v0

v1 whole, which is shorter than its diff:
```python
import functools

import jax
import jax.numpy as jnp
from jax import lax
from jax.experimental import pallas as pl
from jax.experimental.pallas import tpu as pltpu
from jax.sharding import PartitionSpec as P

F32 = jnp.float32
BF16 = jnp.bfloat16
NT = (((1,), (1,)), ((), ()))

FIELDS = 6
SLOTS = 48
VALUES = 8
PEERS = 256
CHUNK = 256


def kernel_weights(offset):
    remain = 1.0 - offset
    return (
        -0.5 * offset * remain * remain,
        1.0 - 2.5 * offset * offset + 1.5 * offset * offset * offset,
        1.0 - 2.5 * remain * remain + 1.5 * remain * remain * remain,
        -0.5 * offset * offset * remain,
    )


def split(value):
    high = value.astype(BF16).astype(F32)
    return high, (value - high).astype(BF16).astype(F32)


def bucket_kernel(fields, frac, owner, slab, line_in, xcell, count, out, key_s, rank_s, place_s, upper_s, acc):
    rows = key_s.shape[0]
    lane = lax.broadcasted_iota(jnp.int32, key_s.shape, 1)
    alive = lane < count[...]
    key = (xcell[...] >> 4) * 8 + slab[...]
    key_s[...] = jnp.where(alive, key, -1).astype(F32)
    place_s[0] = (owner[...] * 8 + (line_in[...] >> 3)).astype(F32)
    place_s[1] = ((((line_in[...] & 7) * 16) + (xcell[...] & 15)) * 256).astype(F32)
    place_s[2], place_s[3] = split(frac[...])
    before = lax.broadcasted_iota(jnp.int32, (CHUNK, CHUNK), 0) < lax.broadcasted_iota(jnp.int32, (CHUNK, CHUNK), 1)
    upper_s[...] = jnp.where(before, 1.0, 0.0).astype(BF16)
    peer = lax.broadcasted_iota(jnp.int32, (PEERS, 128), 0).astype(F32)

    def row_of(ref, row):
        return ref[pl.ds(row, 1), :]

    def hits(row):
        return row_of(key_s, row) == peer

    unroll = 4

    def rank_step(step, base):
        for part in range(unroll):
            row = (step * unroll + part) * 2
            hit = [hits(row + half) for half in range(2)]
            one = jnp.concatenate([jnp.where(h, 1.0, 0.0).astype(BF16) for h in hit], axis=1)
            earlier = jnp.dot(one, upper_s[...], preferred_element_type=F32)
            for half in range(2):
                seen = earlier[:, half * 128:(half + 1) * 128] + base
                rank_s[pl.ds(row + half, 1), :] = jnp.sum(jnp.where(hit[half], seen, 0.0), axis=0, keepdims=True)
            base = base + jnp.dot(one, jnp.ones((CHUNK, 128), BF16), preferred_element_type=F32)
        return base

    lax.fori_loop(0, rows // (2 * unroll), rank_step, jnp.zeros((PEERS, 128), F32))

    slot = lax.broadcasted_iota(jnp.int32, (SLOTS, 128), 0).astype(F32)
    wide = 8
    acc[...] = jnp.zeros_like(acc)

    def send_step(step, carry):
        ones, packed = [], []
        for part in range(wide):
            row = step * wide + part
            ones.append(jnp.where(hits(row), 1.0, 0.0).astype(BF16))
            here = row_of(rank_s, row) == slot
            block = fields[:, pl.ds(pl.multiple_of(row * 128, 128), 128)]
            high, low = split(block)
            highs = [high[f:f + 1] for f in range(FIELDS)]
            lows = [low[f:f + 1] for f in range(FIELDS)]
            highs += [place_s[2, pl.ds(row, 1), :], place_s[0, pl.ds(row, 1), :]]
            lows += [place_s[3, pl.ds(row, 1), :], place_s[1, pl.ds(row, 1), :]]
            packed.append(jnp.concatenate([jnp.where(here, v, 0.0).astype(BF16) for v in highs + lows], axis=0))
        acc[...] += lax.dot_general(
            jnp.concatenate(packed, axis=1), jnp.concatenate(ones, axis=1), NT, preferred_element_type=F32
        )
        return carry

    lax.fori_loop(0, rows // wide, send_step, 0)
    half = VALUES * SLOTS
    total = acc[:half, :] + acc[half:, :]
    out[...] = jnp.swapaxes(total, 0, 1)[:, None, :]


def deposit_kernel(arrived, lattice, low_edge, high_edge, flat_s, weight_s, xin_s, yat_s, zat_s, acc):
    flat_s[...] = jnp.swapaxes(arrived[:, 0, :], 0, 1)
    offset = flat_s[6 * SLOTS:7 * SLOTS, :]
    place = flat_s[7 * SLOTS:8 * SLOTS, :].astype(jnp.int32)
    for number, weight in enumerate(kernel_weights(offset)):
        weight_s[number] = weight
    yat_s[...] = (place & 255).astype(F32)
    xin_s[...] = ((place >> 8) & 15).astype(F32)
    zat_s[...] = (place >> 12).astype(F32)
    acc[...] = jnp.zeros_like(acc)
    sub = lax.broadcasted_iota(jnp.int32, (8, PEERS), 0)
    low_rows = (sub + 1).astype(F32)
    high_rows = (sub + 9).astype(F32)
    edge_rows = jnp.where(sub % 4 == 0, 0, jnp.where(sub % 4 == 3, 99, 16 + sub % 4)).astype(F32)
    first = sub < 4
    y_iota = lax.broadcasted_iota(jnp.int32, (256, PEERS), 0).astype(F32)
    per = 2

    def step(index, carry):
        packed, y_rows, z_rows = [], [], []
        for part in range(per):
            slot = index * per + part
            weights = [weight_s[k, pl.ds(slot, 1), :] for k in range(4)]
            xin = xin_s[pl.ds(slot, 1), :]
            spread = []
            for nodes in (low_rows, high_rows, edge_rows):
                apart = nodes - xin
                value = jnp.zeros((8, PEERS), F32)
                for k in range(4):
                    value = jnp.where(apart == float(k), weights[k], value)
                spread.append(value)
            field = [flat_s[pl.ds(f * SLOTS + slot, 1), :] for f in range(FIELDS)]
            groups = []
            for f in range(FIELDS):
                groups += [spread[0] * field[f], spread[1] * field[f]]
            for f in range(0, FIELDS, 2):
                groups.append(spread[2] * jnp.where(first, field[f], field[f + 1]))
            groups.append(jnp.zeros((8, PEERS), F32))
            whole = jnp.concatenate(groups, axis=0)
            high = whole.astype(BF16)
            low = (whole - high.astype(F32)).astype(BF16)
            packed.append(jnp.concatenate([high, low], axis=0))
            y_rows.append(yat_s[pl.ds(slot, 1), :])
            z_rows.append(zat_s[pl.ds(slot, 1), :])
        values = jnp.concatenate(packed, axis=1)
        for z in range(8):
            one = jnp.concatenate(
                [
                    jnp.where(jnp.where(z_rows[part] == float(z), y_rows[part], -1.0) == y_iota, 1.0, 0.0).astype(BF16)
                    for part in range(per)
                ],
                axis=1,
            )
            acc[z] += lax.dot_general(one, values, NT, preferred_element_type=F32)
        return carry

    lax.fori_loop(0, SLOTS // per, step, 0)
    for z in range(8):
        nodes = jnp.swapaxes(acc[z, :, :128] + acc[z, :, 128:], 0, 1)
        for f in range(FIELDS):
            for half in range(2):
                at = (f * 2 + half) * 8
                lattice[f, half * 8:half * 8 + 8, z, :] = nodes[at:at + 8, :]
            at = 96 + f * 4
            low_edge[f, 0, z:z + 1, :] = nodes[at:at + 1, :]
            high_edge[f, 0, z:z + 1, :] = nodes[at + 1:at + 2, :]
            high_edge[f, 1, z:z + 1, :] = nodes[at + 2:at + 3, :]


def y_kernel(lattice, from_right, from_left, y_offset, y_frac, out):
    width = y_offset.shape[0]

    def one_x(x, halo):
        weights = kernel_weights(y_frac[x])
        shift = y_offset[x]
        is_shift = [shift == s for s in range(-2, 3)]
        factors = []
        for travel in range(-3, 5):
            factor = jnp.zeros_like(weights[0])
            for s in range(-2, 3):
                if -1 <= travel - s <= 2:
                    factor = jnp.where(is_shift[s + 2], weights[travel - s + 1], factor)
            factors.append(factor)
        for f in range(FIELDS):
            values = lattice[f, x]
            if halo is not None:
                values = values + halo[0][f, halo[1]]
            total = values * factors[3]
            for travel in range(-3, 5):
                if travel:
                    total = total + pltpu.roll(values * factors[travel + 3], travel % values.shape[1], 1)
            out[f, x] = total

    one_x(0, (from_left, 0))
    one_x(1, (from_left, 1))
    one_x(width - 1, (from_right, 0))

    def body(x, carry):
        one_x(x, None)
        return carry

    lax.fori_loop(2, width - 1, body, 0)


def params(mib):
    return pltpu.CompilerParams(vmem_limit_bytes=mib << 20)


def bucket(fields, frac, owner, slab, line_in, xcell, count):
    rows = frac.shape[0] // 128
    grid2 = lambda v: v.reshape(rows, 128)
    return pl.pallas_call(
        bucket_kernel,
        out_shape=jax.ShapeDtypeStruct((PEERS, 1, VALUES * SLOTS), F32),
        scratch_shapes=[
            pltpu.VMEM((rows, 128), F32),
            pltpu.VMEM((rows, 128), F32),
            pltpu.VMEM((4, rows, 128), F32),
            pltpu.VMEM((CHUNK, CHUNK), BF16),
            pltpu.VMEM((2 * VALUES * SLOTS, PEERS), F32),
        ],
        compiler_params=params(24),
        name="bucket",
    )(fields, grid2(frac), grid2(owner), grid2(slab), grid2(line_in), grid2(xcell), count.reshape(rows, 1))


def deposit(arrived):
    return pl.pallas_call(
        deposit_kernel,
        out_shape=(
            jax.ShapeDtypeStruct((FIELDS, 16, 8, 256), F32),
            jax.ShapeDtypeStruct((FIELDS, 1, 8, 256), F32),
            jax.ShapeDtypeStruct((FIELDS, 2, 8, 256), F32),
        ),
        scratch_shapes=[
            pltpu.VMEM((VALUES * SLOTS, PEERS), F32),
            pltpu.VMEM((4, SLOTS, PEERS), F32),
            pltpu.VMEM((SLOTS, PEERS), F32),
            pltpu.VMEM((SLOTS, PEERS), F32),
            pltpu.VMEM((SLOTS, PEERS), F32),
            pltpu.VMEM((8, 256, 256), F32),
        ],
        compiler_params=params(24),
        name="deposit",
    )(arrived)


def y_pass(lattice, from_right, from_left, y_offset, y_frac):
    return pl.pallas_call(
        y_kernel,
        out_shape=jax.ShapeDtypeStruct(lattice.shape, F32),
        compiler_params=params(16),
        name="y_pass",
    )(lattice, from_right, from_left, y_offset, y_frac)


def per_device(fields, frac_x, owner, slab, line_in, xcell, tile_count, y_offset, y_frac):
    lines = lax.axis_size("lines")
    outgoing = bucket(fields, frac_x, owner, slab, line_in, xcell, tile_count)
    arrived = lax.all_to_all(outgoing, ("lines", "slab"), split_axis=0, concat_axis=0, tiled=True)
    lattice, low_edge, high_edge = deposit(arrived)
    from_left = lax.ppermute(high_edge, "lines", [(i, (i + 1) % lines) for i in range(lines)])
    from_right = lax.ppermute(low_edge, "lines", [(i, (i - 1) % lines) for i in range(lines)])
    return y_pass(lattice, from_right, from_left, y_offset, y_frac)


def solution(mesh):
    return jax.shard_map(
        per_device,
        mesh=mesh,
        in_specs=(
            P(None, ("lines", "slab")),
            P(("lines", "slab")),
            P(("lines", "slab")),
            P(("lines", "slab")),
            P(("lines", "slab")),
            P(("lines", "slab")),
            P(("lines", "slab")),
            P("lines", "slab", None),
            P("lines", "slab", None),
        ),
        out_specs=P(None, "lines", "slab", None),
        check_vma=False,
    )
```

time: 807 us -> 77.9 us (0.10); the launches traced: 795 us -> 77.5 us
  local copies, waits for them, and re-layouts: 369 us -> 4.76 us
  other arithmetic: 344 us -> 0 us
  waiting for transfers between devices: 37.5 us -> 3.32 us
  Pallas kernels: 0 us -> 30.8 us
  starting transfers between devices: 22.2 us -> 4.86 us
  blocking collectives: 20.5 us -> 33.7 us
    scatter-add x1 -> x0, other arithmetic: 279 us -> none  [deposit(): jnp.zeros((carried.shape[0], cells), jnp.float32).at[:, landing_cells]]
    gather x21 -> x0, local copies, waits for them, and re-layouts: 174 us -> none  [the longest x1 51 us: send_particles(): starts[jnp.minimum(sorted_key, targets - 1)]]
    scatter x2 -> x0, local copies, waits for them, and re-layouts: 100 us -> none  [the longest x1 69.6 us: send_particles(): floats_out.at[:, slot_index].set(payload[:, sort_order], mode='drop')]
    all_to_all x4 -> x0, waiting for transfers between devices: 37.5 us -> none  [the longest x1 19.3 us: per_device(): lax.all_to_all(deposited, 'lines', split_axis=3, concat_axis=2, tiled=True)]
    select_n x19 -> x0, other arithmetic: 37.4 us -> none  [the longest x1 36.7 us: send_particles(): sort_key = jnp.where(alive_slot, target, targets)]
    reshape x4 -> x1, local copies, waits for them, and re-layouts: 35.9 us -> 0.1 us  [bucket(): count.reshape(rows, 1)]
    pallas_call x0 -> x3, Pallas kernels: none -> 30.8 us  [the longest x1 18.8 us: deposit(): pl.pallas_call(deposit_kernel, out_shape=(jax.ShapeDtypeStruct((FIELDS, 1...]
    all_to_all x4 -> x0, starting transfers between devices: 22.2 us -> none  [the longest x1 6.55 us: send_particles(): lax.all_to_all(lax.all_to_all(cells_out, 'lines', split_axis=1, concat_ax...]
  transfers between devices with their start and end apart: 4 -> 2, of which waited for: 3 -> 2; matrix products, arithmetic and copies ran while one was open for 10% -> 0% of each run, Pallas kernels for 0% -> 0%
where the time goes in v1:
time: 77.9 us; the launch traced here: 77.5 us
  blocking collectives  33.7 us (43%)
  Pallas kernels  30.8 us (40%)
  starting transfers between devices  4.86 us (6%)
  local copies, waits for them, and re-layouts  4.76 us (6%)
  waiting for transfers between devices  3.32 us (4%)
    all_to_all x1, blocking collectives, per_device(): lax.all_to_all(outgoing, ('lines', 'slab'), split_axis=0, concat_axis=0,...  33.7 us
    pallas_call x1, Pallas kernels, deposit(): pl.pallas_call(deposit_kernel, out_shape=(jax.ShapeDtypeStruct((FIELDS, 1...  18.8 us
    pallas_call x1, Pallas kernels, bucket(): pl.pallas_call(bucket_kernel, out_shape=jax.ShapeDtypeStruct((PEERS, 1, V...  8.63 us
    unnamed x18, local copies, waits for them, and re-layouts  4.66 us
    ppermute x1, starting transfers between devices, per_device(): lax.ppermute(low_edge, 'lines', [(i, (i - 1) % lines) for i in range(line...  4.04 us
    pallas_call x1, Pallas kernels, y_pass(): pl.pallas_call(y_kernel, out_shape=jax.ShapeDtypeStruct(lattice.shape, F3...  3.37 us
    ppermute x1, waiting for transfers between devices, per_device(): lax.ppermute(high_edge, 'lines', [(i, (i + 1) % lines) for i in range(lin...  2.03 us
  transfers between devices with their start and end apart: 2, of which 2 were waited for; matrix products, arithmetic and copies ran while one was open for 0% of the time, Pallas kernels for 0%

profile of v1, /device:TPU:1, one launch (start us, length us, event | category | flops | bytes accessed | tf_op | source)
XLA Modules:
  0.0 77.5 jit_solution(17028064443720385100)
XLA Ops:
  0.0 0.0 copy-start.8
  0.0 0.0 copy-start.3
  0.0 0.7 copy-done.8
  0.7 0.1 copy.10.count
  0.8 0.0 copy-done.3
  0.8 0.0 copy-start
  0.8 0.9 %copy-done = f32[6,8192]{1,0:T(8,128)S(1)} copy-done((f32[6,8192]{1,0:T(8,128)S(1)}, f32[6,8192]{1,0:T(8,128)}, u32[]{:S(2)}) %copy-start) | copy-done | bytes 196632
  1.7 0.0 copy-start.4
  1.7 0.8 copy-done.4
  2.5 0.0 copy-start.5
  2.5 0.8 copy-done.5
  3.2 0.0 copy-start.6
  3.2 0.8 copy-done.6
  4.0 0.0 copy-start.7
  4.0 0.8 copy-done.7
  4.8 8.6 %bucket.1 = f32[256,1,384]{2,1,0:T(1,128)S(1)} custom-call(f32[6,8192]{1,0:T(8,128)S(1)} %copy-done, f32[64,128]{1,0:T(8,128)S(1)} %bitcast.6, s32[64,128]{1,0:T(8,128)S(1)} %bitcast.7, s32[64,128]{1,0:T(8,128)S(1)} %bitcast.8, s32[64,128]{1,0:T(8,128)S(1)} %bitcast.9, s32[64,128]{1,0:T(8,128)S(1)} %bitcast.10, s32[64,1]{1,0:T(8,128)S(1)} %copy.10.count), custom_call_target="tpu_custom_call" | custom-call | tf_op jit(solution)/shard_map/bucket/pallas_call | solution.py:210
  13.4 33.7 %all_to_all.5.arrived = f32[256,1,384]{2,1,0:T(1,128)S(1)} all-to-all(f32[256,1,384]{2,1,0:T(1,128)S(1)} %bucket.1), channel_id=1, replica_groups=mesh['lines'=32,'slab'=8] {'lines','slab'}, dimensions={0} | all-to-all | bytes 786432 | tf_op jit(solution)/shard_map/all_to_all | solution.py:258
  47.1 0.0 copy-start.1
  47.1 0.0 copy-start.2
  47.1 18.8 %deposit.1 = (f32[6,16,8,256]{3,2,1,0:T(8,128)S(1)}, f32[6,1,8,256]{3,2,1,0:T(8,128)S(1)}, f32[6,2,8,256]{3,2,1,0:T(8,128)S(1)}) custom-call(f32[256,1,384]{2,1,0:T(1,128)S(1)} %all_to_all.5.arrived), custom_call_target="tpu_custom_call" | custom-call | tf_op jit(solution)/shard_map/deposit/pallas_call | solution.py:226
  65.9 0.8 %collective-permute-start.1 = (f32[6,2,8,256]{3,2,1,0:T(8,128)S(1)}, f32[6,2,8,256]{3,2,1,0:T(8,128)S(1)}, u32[]{:S(2)}, u32[]{:S(2)}) collective-permute-start(f32[6,2,8,256]{3,2,1,0:T(8,128)S(1)} %get-tuple-element.10), channel_id=1, source_target_pairs={{0,8},{8,16},{16,24},{24,32},{32,40},{40,48},{48,56},{56,64},{64,7... | collective-permute-start | bytes 294920 | tf_op jit(solution)/shard_map/ppermute | solution.py:260
  66.7 4.0 %collective-permute-start = (f32[6,1,8,256]{3,2,1,0:T(8,128)S(1)}, f32[6,1,8,256]{3,2,1,0:T(8,128)S(1)}, u32[]{:S(2)}, u32[]{:S(2)}) collective-permute-start(f32[6,1,8,256]{3,2,1,0:T(8,128)S(1)} %get-tuple-element.9), channel_id=1, source_target_pairs={{0,248},{8,0},{16,8},{24,16},{32,24},{40,32},{48,40},{56,48},{64,5... | collective-permute-start | bytes 147464 | tf_op jit(solution)/shard_map/ppermute | solution.py:261
  70.8 1.3 %collective-permute-done.from_right = f32[6,1,8,256]{3,2,1,0:T(8,128)S(1)} collective-permute-done((f32[6,1,8,256]{3,2,1,0:T(8,128)S(1)}, f32[6,1,8,256]{3,2,1,0:T(8,128)S(1)}, u32[]{:S(2)}, u32[]{:S(2)}) %collective-permute-start) | collective-permute-done | bytes 49184 | tf_op jit(solution)/shard_map/ppermute | solution.py:261
  72.1 2.0 %collective-permute-done.1.from_left = f32[6,2,8,256]{3,2,1,0:T(8,128)S(1)} collective-permute-done((f32[6,2,8,256]{3,2,1,0:T(8,128)S(1)}, f32[6,2,8,256]{3,2,1,0:T(8,128)S(1)}, u32[]{:S(2)}, u32[]{:S(2)}) %collective-permute-start.1) | collective-permute-done | bytes 98336 | tf_op jit(solution)/shard_map/ppermute | solution.py:260
  74.1 0.0 copy-done.1
  74.1 0.0 copy-done.2
  74.1 3.4 %y_pass.1 = f32[6,16,8,256]{3,2,1,0:T(8,128)} custom-call(f32[6,16,8,256]{3,2,1,0:T(8,128)S(1)} %get-tuple-element.8.lattice, f32[6,1,8,256]{3,2,1,0:T(8,128)S(1)} %collective-permute-done.from_right, f32[6,2,8,256]{3,2,1,0:T(8,128)S(1)} %collective-permute-done.1.from_left, s32[16,8,256]{2,1,0:T(8,128)S(1)} %copy-done.1, f32[16,8,256]{2,1,0:T(8,128)S(1)} %copy-done.2), custom_call_target="tpu_custom_call" | custom-call | tf_op jit(solution)/shard_map/y_pass/pallas_call | solution.py:247
Async XLA Ops:
  0.0 0.7 copy-start.8
  0.0 0.8 copy-start.3
  0.8 0.9 %copy-start = (f32[6,8192]{1,0:T(8,128)S(1)}, f32[6,8192]{1,0:T(8,128)}, u32[]{:S(2)}) copy-start(f32[6,8192]{1,0:T(8,128)} %fields.1) | copy-start | bytes 589828
  1.7 0.8 copy-start.4
  2.5 0.8 copy-start.5
  3.2 0.8 copy-start.6
  4.0 0.8 copy-start.7
  47.1 27.0 %copy-start.1 = (s32[16,8,256]{2,1,0:T(8,128)S(1)}, s32[16,8,256]{2,1,0:T(8,128)}, u32[]{:S(2)}) copy-start(s32[16,8,256]{2,1,0:T(8,128)} %y_offset.1) | copy-start | bytes 393220
  47.1 27.0 %copy-start.2 = (f32[16,8,256]{2,1,0:T(8,128)S(1)}, f32[16,8,256]{2,1,0:T(8,128)}, u32[]{:S(2)}) copy-start(f32[16,8,256]{2,1,0:T(8,128)} %y_frac.1) | copy-start | bytes 393220
  65.9 8.2 %collective-permute-start.1 = (f32[6,2,8,256]{3,2,1,0:T(8,128)S(1)}, f32[6,2,8,256]{3,2,1,0:T(8,128)S(1)}, u32[]{:S(2)}, u32[]{:S(2)}) collective-permute-start(f32[6,2,8,256]{3,2,1,0:T(8,128)S(1)} %get-tuple-element.10), channel_id=1, source_target_pairs={{0,8},{8,16},{16,24},{24,32},{32,40},{40,48},{48,56},{56,64},{64,7... | collective-permute-start | bytes 294920 | tf_op jit(solution)/shard_map/ppermute | solution.py:260
  66.7 5.3 %collective-permute-start = (f32[6,1,8,256]{3,2,1,0:T(8,128)S(1)}, f32[6,1,8,256]{3,2,1,0:T(8,128)S(1)}, u32[]{:S(2)}, u32[]{:S(2)}) collective-permute-start(f32[6,1,8,256]{3,2,1,0:T(8,128)S(1)} %get-tuple-element.9), channel_id=1, source_target_pairs={{0,248},{8,0},{16,8},{24,16},{32,24},{40,32},{48,40},{56,48},{64,5... | collective-permute-start | bytes 147464 | tf_op jit(solution)/shard_map/ppermute | solution.py:261

commit v2 on v1

v2 whole, which is shorter than its diff:
```python
import functools

import jax
import jax.numpy as jnp
from jax import lax
from jax.experimental import pallas as pl
from jax.experimental.pallas import tpu as pltpu
from jax.sharding import PartitionSpec as P

F32 = jnp.float32
BF16 = jnp.bfloat16
NT = (((1,), (1,)), ((), ()))

FIELDS = 6
SLOTS = 48
VALUES = 8
PEERS = 256
CHUNK = 256
PLANES = 8
OWN = 8


def kernel_weights(offset):
    remain = 1.0 - offset
    return (
        -0.5 * offset * remain * remain,
        1.0 - 2.5 * offset * offset + 1.5 * offset * offset * offset,
        1.0 - 2.5 * remain * remain + 1.5 * remain * remain * remain,
        -0.5 * offset * offset * remain,
    )


def split(value):
    high = value.astype(BF16).astype(F32)
    return high, (value - high).astype(BF16).astype(F32)


def bucket_kernel(
    fields_h, frac_h, owner_h, slab_h, line_in_h, xcell_h, count_h, out,
    fields, frac, owner, slab, line_in, xcell, count, sems, key_s, rank_s, place_s, upper_s, acc,
):
    moves = [
        pltpu.make_async_copy(source, goal, sems.at[number])
        for number, (source, goal) in enumerate((
            (count_h, count), (slab_h, slab), (xcell_h, xcell), (owner_h, owner), (line_in_h, line_in), (frac_h, frac), (fields_h, fields),
        ))
    ]
    for move in moves:
        move.start()
    for move in moves:
        move.wait()
    rows = key_s.shape[0]
    lane = lax.broadcasted_iota(jnp.int32, key_s.shape, 1)
    tile = lax.broadcasted_iota(jnp.int32, (rows, rows), 0) == lax.broadcasted_iota(jnp.int32, (rows, rows), 1)
    alive = lane < jnp.sum(jnp.where(tile, count[...], 0), axis=1, keepdims=True)
    key = (xcell[...] >> 4) * 8 + slab[...]
    key_s[...] = jnp.where(alive, key, -1).astype(F32)
    place_s[0] = (owner[...] * 8 + (line_in[...] >> 3)).astype(F32)
    place_s[1] = ((128 + (line_in[...] & 7) * 16 + (xcell[...] & 15)) * 256).astype(F32)
    place_s[2], place_s[3] = split(frac[...])
    before = lax.broadcasted_iota(jnp.int32, (CHUNK, CHUNK), 0) < lax.broadcasted_iota(jnp.int32, (CHUNK, CHUNK), 1)
    upper_s[...] = jnp.where(before, 1.0, 0.0).astype(BF16)
    peer = lax.broadcasted_iota(jnp.int32, (PEERS, 128), 0).astype(F32)

    def row_of(ref, row):
        return ref[pl.ds(row, 1), :]

    def hits(row):
        return row_of(key_s, row) == peer

    unroll = 4

    def rank_step(step, base):
        for part in range(unroll):
            row = (step * unroll + part) * 2
            hit = [hits(row + half) for half in range(2)]
            one = jnp.concatenate([jnp.where(h, 1.0, 0.0).astype(BF16) for h in hit], axis=1)
            earlier = jnp.dot(one, upper_s[...], preferred_element_type=F32)
            for half in range(2):
                seen = earlier[:, half * 128:(half + 1) * 128] + base
                rank_s[pl.ds(row + half, 1), :] = jnp.sum(jnp.where(hit[half], seen, 0.0), axis=0, keepdims=True)
            base = base + jnp.dot(one, jnp.ones((CHUNK, 128), BF16), preferred_element_type=F32)
        return base

    lax.fori_loop(0, rows // (2 * unroll), rank_step, jnp.zeros((PEERS, 128), F32))

    slot = lax.broadcasted_iota(jnp.int32, (SLOTS, 128), 0).astype(F32)
    wide = 8
    acc[...] = jnp.zeros_like(acc)

    def send_step(step, carry):
        ones, packed = [], []
        for part in range(wide):
            row = step * wide + part
            ones.append(jnp.where(hits(row), 1.0, 0.0).astype(BF16))
            here = row_of(rank_s, row) == slot
            block = fields[:, pl.ds(pl.multiple_of(row * 128, 128), 128)]
            high, low = split(block)
            highs = [high[f:f + 1] for f in range(FIELDS)]
            lows = [low[f:f + 1] for f in range(FIELDS)]
            highs += [place_s[2, pl.ds(row, 1), :], place_s[0, pl.ds(row, 1), :]]
            lows += [place_s[3, pl.ds(row, 1), :], place_s[1, pl.ds(row, 1), :]]
            packed.append(jnp.concatenate([jnp.where(here, v, 0.0).astype(BF16) for v in highs + lows], axis=0))
        acc[...] += lax.dot_general(
            jnp.concatenate(packed, axis=1), jnp.concatenate(ones, axis=1), NT, preferred_element_type=F32
        )
        return carry

    lax.fori_loop(0, rows // wide, send_step, 0)
    half = VALUES * SLOTS
    total = acc[:half, :] + acc[half:, :]
    out[...] = jnp.swapaxes(total, 0, 1)[:, None, :]


def deposit_kernel(arrived, lattice, low_edge, high_edge, flat_s, plane_s, to_s, over_s, mine_s, weight_s, acc):
    flat_s[...] = jnp.swapaxes(arrived[:, 0, :], 0, 1)
    place = flat_s[7 * SLOTS:8 * SLOTS, :].astype(jnp.int32)
    live = place >= 32768
    plane = jnp.where(live, (place >> 12) & 7, 99).astype(F32)
    plane_s[...] = plane
    sub = lax.broadcasted_iota(jnp.int32, (8, PEERS), 0)
    subf = sub.astype(F32)
    seen = jnp.zeros((PLANES, PEERS), F32)
    for slot in range(SLOTS):
        hit = plane_s[slot:slot + 1, :] == subf
        to_s[slot:slot + 1, :] = jnp.sum(jnp.where(hit, seen, 0.0), axis=0, keepdims=True)
        seen = seen + jnp.where(hit, 1.0, 0.0)
    rank = to_s[...]
    fits = rank < OWN
    to_s[...] = jnp.where(fits, plane * OWN + rank, 9999.0)
    extra = jnp.logical_and(live, jnp.logical_not(fits))
    before = lax.broadcasted_iota(jnp.int32, (SLOTS, SLOTS), 1) < lax.broadcasted_iota(jnp.int32, (SLOTS, SLOTS), 0)
    order = jnp.dot(jnp.where(before, 1.0, 0.0).astype(BF16), jnp.where(extra, 1.0, 0.0).astype(BF16), preferred_element_type=F32)
    over_s[...] = jnp.where(extra, order, -1.0)
    rounds = jnp.max(jnp.where(extra, order, -1.0)).astype(jnp.int32) + 1

    low_rows = (sub + 1).astype(F32)
    high_rows = (sub + 9).astype(F32)
    edge_rows = jnp.where(sub % 4 == 0, 0, jnp.where(sub % 4 == 3, 99, 16 + sub % 4)).astype(F32)
    first = sub < 4
    y_iota = lax.broadcasted_iota(jnp.int32, (256, PEERS), 0).astype(F32)

    def rows_of(weights, xin, field):
        spread = []
        for nodes in (low_rows, high_rows, edge_rows):
            apart = nodes - xin
            value = jnp.zeros((8, PEERS), F32)
            for k in range(4):
                value = jnp.where(apart == float(k), weights[k], value)
            spread.append(value)
        groups = []
        for f in range(FIELDS):
            groups += [spread[0] * field[f], spread[1] * field[f]]
        for f in range(0, FIELDS, 2):
            groups.append(spread[2] * jnp.where(first, field[f], field[f + 1]))
        groups.append(jnp.zeros((8, PEERS), F32))
        whole = jnp.concatenate(groups, axis=0)
        high = whole.astype(BF16)
        low = (whole - high.astype(F32)).astype(BF16)
        return jnp.concatenate([high, low], axis=0)

    def planes_step(step, carry):
        pair = 2
        found = [[jnp.zeros((8, PEERS), F32) for _ in range(VALUES)] for _ in range(pair)]
        goal = [subf + ((step * pair + part) * OWN).astype(F32) for part in range(pair)]
        for slot in range(SLOTS):
            to = to_s[slot:slot + 1, :]
            rows = [flat_s[v * SLOTS + slot:v * SLOTS + slot + 1, :] for v in range(VALUES)]
            for part in range(pair):
                hit = to == goal[part]
                found[part] = [jnp.where(hit, rows[v], found[part][v]) for v in range(VALUES)]
        for part in range(pair):
            spot = found[part][7].astype(jnp.int32)
            for v in range(FIELDS):
                mine_s[part, v] = found[part][v]
            mine_s[part, 6] = ((spot >> 8) & 15).astype(F32)
            mine_s[part, 7] = (spot & 255).astype(F32)
            for number, weight in enumerate(kernel_weights(found[part][6])):
                weight_s[part, number] = weight
        for part in range(pair):
            packed, ones = [], []
            for own in range(OWN):
                row = lambda v: mine_s[part, v, own:own + 1, :]
                packed.append(rows_of([weight_s[part, k, own:own + 1, :] for k in range(4)], row(6), [row(f) for f in range(FIELDS)]))
                ones.append(jnp.where(row(7) == y_iota, 1.0, 0.0).astype(BF16))
            acc[step * pair + part] = lax.dot_general(
                jnp.concatenate(ones, axis=1), jnp.concatenate(packed, axis=1), NT, preferred_element_type=F32
            )
        return carry

    lax.fori_loop(0, PLANES // 2, planes_step, 0)

    def extra_step(number, carry):
        hit = over_s[...] == number.astype(F32)
        pick = lambda v: jnp.sum(jnp.where(hit, flat_s[v * SLOTS:(v + 1) * SLOTS, :], 0.0), axis=0, keepdims=True)
        field = [pick(f) for f in range(FIELDS)]
        weights = kernel_weights(pick(6))
        spot = pick(7).astype(jnp.int32)
        packed = rows_of(weights, ((spot >> 8) & 15).astype(F32), field)
        plane = (spot >> 12) & 7
        spot_y = (spot & 255).astype(F32)
        for z in range(PLANES):
            one = jnp.where(jnp.where(plane == z, spot_y, -1.0) == y_iota, 1.0, 0.0).astype(BF16)
            acc[z] += lax.dot_general(one, packed, NT, preferred_element_type=F32)
        return carry

    lax.fori_loop(0, rounds, extra_step, 0)
    for z in range(PLANES):
        nodes = jnp.swapaxes(acc[z, :, :128] + acc[z, :, 128:], 0, 1)
        for f in range(FIELDS):
            for half in range(2):
                at = (f * 2 + half) * 8
                lattice[f, half * 8:half * 8 + 8, z, :] = nodes[at:at + 8, :]
            at = 96 + f * 4
            low_edge[f, 0, z:z + 1, :] = nodes[at:at + 1, :]
            high_edge[f, 0, z:z + 1, :] = nodes[at + 1:at + 2, :]
            high_edge[f, 1, z:z + 1, :] = nodes[at + 2:at + 3, :]


def y_factors(y_offset, y_frac):
    weights = kernel_weights(y_frac)
    is_shift = [y_offset == s for s in range(-2, 3)]
    factors = []
    for travel in range(-3, 5):
        factor = jnp.zeros_like(weights[0])
        for s in range(-2, 3):
            if -1 <= travel - s <= 2:
                factor = jnp.where(is_shift[s + 2], weights[travel - s + 1], factor)
        factors.append(factor)
    return factors


def y_spread(values, factors):
    total = values * factors[3]
    for travel in range(-3, 5):
        if travel:
            total = total + pltpu.roll(values * factors[travel + 3], travel % values.shape[1], 1)
    return total


def y_inner_kernel(lattice, y_offset, y_frac, out, ready, sems):
    width = y_offset.shape[0]

    def body(x, carry):
        factors = y_factors(y_offset[x], y_frac[x])
        for f in range(FIELDS):
            ready[x, f] = y_spread(lattice[f, x], factors)
        pltpu.make_async_copy(ready.at[x], out.at[:, x], sems.at[x]).start()
        return carry

    lax.fori_loop(2, width - 1, body, 0)

    def drain(x, carry):
        pltpu.make_async_copy(ready.at[x], out.at[:, x], sems.at[x]).wait()
        return carry

    lax.fori_loop(2, width - 1, drain, 0)


def y_edge_kernel(lattice, from_right, from_left, y_offset, y_frac, partial, out, ready, sems):
    width = y_offset.shape[0]
    moves = []
    for number, (x, halo, at) in enumerate(((0, from_left, 0), (1, from_left, 1), (width - 1, from_right, 0))):
        factors = y_factors(y_offset[x], y_frac[x])
        for f in range(FIELDS):
            ready[f, number] = y_spread(lattice[f, x] + halo[f, at], factors)
        moves.append(pltpu.make_async_copy(ready.at[:, number], out.at[:, x], sems.at[number]))
        moves[-1].start()
    for move in moves:
        move.wait()


def params(mib):
    return pltpu.CompilerParams(vmem_limit_bytes=mib << 20)


def bucket(fields, frac, owner, slab, line_in, xcell, count):
    rows = frac.shape[0] // 128
    grid2 = lambda v: v.reshape(rows, 128)
    return pl.pallas_call(
        bucket_kernel,
        out_shape=jax.ShapeDtypeStruct((PEERS, 1, VALUES * SLOTS), F32),
        in_specs=[pl.BlockSpec(memory_space=pltpu.HBM)] * 7,
        scratch_shapes=[
            pltpu.VMEM(fields.shape, F32),
            pltpu.VMEM((rows, 128), F32),
            pltpu.VMEM((rows, 128), jnp.int32),
            pltpu.VMEM((rows, 128), jnp.int32),
            pltpu.VMEM((rows, 128), jnp.int32),
            pltpu.VMEM((rows, 128), jnp.int32),
            pltpu.VMEM((1, rows), jnp.int32),
            pltpu.SemaphoreType.DMA((7,)),
            pltpu.VMEM((rows, 128), F32),
            pltpu.VMEM((rows, 128), F32),
            pltpu.VMEM((4, rows, 128), F32),
            pltpu.VMEM((CHUNK, CHUNK), BF16),
            pltpu.VMEM((2 * VALUES * SLOTS, PEERS), F32),
        ],
        compiler_params=params(56),
        name="bucket",
    )(fields, grid2(frac), grid2(owner), grid2(slab), grid2(line_in), grid2(xcell), count.reshape(1, rows))


def deposit(arrived):
    return pl.pallas_call(
        deposit_kernel,
        out_shape=(
            jax.ShapeDtypeStruct((FIELDS, 16, 8, 256), F32),
            jax.ShapeDtypeStruct((FIELDS, 1, 8, 256), F32),
            jax.ShapeDtypeStruct((FIELDS, 2, 8, 256), F32),
        ),
        scratch_shapes=[
            pltpu.VMEM((VALUES * SLOTS, PEERS), F32),
            pltpu.VMEM((SLOTS, PEERS), F32),
            pltpu.VMEM((SLOTS, PEERS), F32),
            pltpu.VMEM((SLOTS, PEERS), F32),
            pltpu.VMEM((2, VALUES, 8, PEERS), F32),
            pltpu.VMEM((2, 4, 8, PEERS), F32),
            pltpu.VMEM((8, 256, 256), F32),
        ],
        compiler_params=params(24),
        name="deposit",
    )(arrived)


def y_inner(lattice, y_offset, y_frac):
    return pl.pallas_call(
        y_inner_kernel,
        out_shape=jax.ShapeDtypeStruct(lattice.shape, F32),
        out_specs=pl.BlockSpec(memory_space=pltpu.HBM),
        scratch_shapes=[
            pltpu.VMEM((lattice.shape[1], FIELDS) + lattice.shape[2:], F32),
            pltpu.SemaphoreType.DMA((lattice.shape[1],)),
        ],
        compiler_params=params(16),
        cost_estimate=pl.CostEstimate(flops=20 * lattice.size, bytes_accessed=8 * lattice.size, transcendentals=0),
        name="y_inner",
    )(lattice, y_offset, y_frac)


def y_edge(lattice, from_right, from_left, y_offset, y_frac, partial):
    vmem = pl.BlockSpec(memory_space=pltpu.VMEM)
    return pl.pallas_call(
        y_edge_kernel,
        out_shape=jax.ShapeDtypeStruct(lattice.shape, F32),
        in_specs=[vmem] * 5 + [pl.BlockSpec(memory_space=pltpu.HBM)],
        out_specs=pl.BlockSpec(memory_space=pltpu.HBM),
        input_output_aliases={5: 0},
        scratch_shapes=[
            pltpu.VMEM((FIELDS, 3) + lattice.shape[2:], F32),
            pltpu.SemaphoreType.DMA((3,)),
        ],
        compiler_params=params(16),
        name="y_edge",
    )(lattice, from_right, from_left, y_offset, y_frac, partial)


def per_device(fields, frac_x, owner, slab, line_in, xcell, tile_count, y_offset, y_frac):
    lines = lax.axis_size("lines")
    outgoing = bucket(fields, frac_x, owner, slab, line_in, xcell, tile_count)
    arrived = lax.all_to_all(outgoing, ("lines", "slab"), split_axis=0, concat_axis=0, tiled=True)
    lattice, low_edge, high_edge = deposit(arrived)
    from_left = lax.ppermute(high_edge, "lines", [(i, (i + 1) % lines) for i in range(lines)])
    from_right = lax.ppermute(low_edge, "lines", [(i, (i - 1) % lines) for i in range(lines)])
    partial = y_inner(lattice, y_offset, y_frac)
    return y_edge(lattice, from_right, from_left, y_offset, y_frac, partial)


def solution(mesh):
    return jax.shard_map(
        per_device,
        mesh=mesh,
        in_specs=(
            P(None, ("lines", "slab")),
            P(("lines", "slab")),
            P(("lines", "slab")),
            P(("lines", "slab")),
            P(("lines", "slab")),
            P(("lines", "slab")),
            P(("lines", "slab")),
            P("lines", "slab", None),
            P("lines", "slab", None),
        ),
        out_specs=P(None, "lines", "slab", None),
        check_vma=False,
    )
```

time: 77.9 us -> 61 us (0.78)
  Pallas kernels: 30.8 us -> 21.7 us
  local copies, waits for them, and re-layouts: 4.76 us -> 0.01 us
  waiting for transfers between devices: 3.32 us -> 0.38 us
    pallas_call x1, Pallas kernels: 18.8 us -> 7.24 us  [deposit(): pl.pallas_call(deposit_kernel, out_shape=(jax.ShapeDtypeStruct((FIELDS, 1...]
    unnamed x18 -> x4, local copies, waits for them, and re-layouts: 4.66 us -> 0.01 us
    pallas_call x1, Pallas kernels: 8.63 us -> 10.6 us  [bucket(): pl.pallas_call(bucket_kernel, out_shape=jax.ShapeDtypeStruct((PEERS, 1, V...]
    ppermute x1, waiting for transfers between devices: 2.03 us -> 0.38 us  [per_device(): lax.ppermute(high_edge, 'lines', [(i, (i + 1) % lines) for i in range(lin...]
    ppermute x1, waiting for transfers between devices: 1.29 us -> 0.01 us  [per_device(): lax.ppermute(low_edge, 'lines', [(i, (i - 1) % lines) for i in range(line...]
    pallas_call x1 -> x2, Pallas kernels: 3.37 us -> 3.91 us  [the longest x1 2.92 us: y_inner(): pl.pallas_call(y_inner_kernel, out_shape=jax.ShapeDtypeStruct(lattice.sha...]
  transfers between devices with their start and end apart: 2 -> 2, of which waited for: 2 -> 1; matrix products, arithmetic and copies ran while one was open for 0% -> 0% of each run, Pallas kernels for 0% -> 5%
where the time goes in v2:
time: 61 us; the launch traced here: 60.9 us
  blocking collectives  33.9 us (56%)
  Pallas kernels  21.7 us (36%)
  starting transfers between devices  4.86 us (8%)
    all_to_all x1, blocking collectives, per_device(): lax.all_to_all(outgoing, ('lines', 'slab'), split_axis=0, concat_axis=0,...  33.9 us
    pallas_call x1, Pallas kernels, bucket(): pl.pallas_call(bucket_kernel, out_shape=jax.ShapeDtypeStruct((PEERS, 1, V...  10.6 us
    pallas_call x1, Pallas kernels, deposit(): pl.pallas_call(deposit_kernel, out_shape=(jax.ShapeDtypeStruct((FIELDS, 1...  7.24 us
    ppermute x1, starting transfers between devices, per_device(): lax.ppermute(low_edge, 'lines', [(i, (i - 1) % lines) for i in range(line...  4.58 us
    pallas_call x1, Pallas kernels, y_inner(): pl.pallas_call(y_inner_kernel, out_shape=jax.ShapeDtypeStruct(lattice.sha...  2.92 us
  transfers between devices with their start and end apart: 2, of which 1 were waited for; matrix products, arithmetic and copies ran while one was open for 0% of the time, Pallas kernels for 5%

profile of v2, /device:TPU:1, one launch (start us, length us, event | category | flops | bytes accessed | tf_op | source)
XLA Modules:
  0.0 60.9 jit_solution(3731575460451219948)
XLA Ops:
  0.0 10.6 %bucket.1 = f32[256,1,384]{2,1,0:T(1,128)} custom-call(f32[6,8192]{1,0:T(8,128)} %fields_h.1, f32[64,128]{1,0:T(8,128)} %bitcast.6, s32[64,128]{1,0:T(8,128)} %bitcast.7, s32[64,128]{1,0:T(8,128)} %bitcast.8, s32[64,128]{1,0:T(8,128)} %bitcast.9, s32[64,128]{1,0:T(8,128)} %bitcast.10, s32[1,64]{1,0:T(1,128)} %bitcast.11), custom_call_target="tpu_custom_call" | custom-call | tf_op jit(solution)/shard_map/bucket/pallas_call | solution.py:280
  10.6 33.9 %all_to_all.5.arrived = f32[256,1,384]{2,1,0:T(1,128)S(1)} all-to-all(f32[256,1,384]{2,1,0:T(1,128)} %bucket.1), channel_id=1, replica_groups=mesh['lines'=32,'slab'=8] {'lines','slab'}, dimensions={0} | all-to-all | bytes 786432 | tf_op jit(solution)/shard_map/all_to_all | solution.py:361
  44.4 0.0 copy-start
  44.5 0.0 copy-start.1
  44.5 7.2 %deposit.1 = (f32[6,16,8,256]{3,2,1,0:T(8,128)S(1)}, f32[6,1,8,256]{3,2,1,0:T(8,128)S(1)}, f32[6,2,8,256]{3,2,1,0:T(8,128)S(1)}) custom-call(f32[256,1,384]{2,1,0:T(1,128)S(1)} %all_to_all.5.arrived), custom_call_target="tpu_custom_call" | custom-call | tf_op jit(solution)/shard_map/deposit/pallas_call | solution.py:305
  51.7 0.3 collective-permute-start.1
  52.0 4.6 %collective-permute-start = (f32[6,1,8,256]{3,2,1,0:T(8,128)S(1)}, f32[6,1,8,256]{3,2,1,0:T(8,128)S(1)}, u32[]{:S(2)}, u32[]{:S(2)}) collective-permute-start(f32[6,1,8,256]{3,2,1,0:T(8,128)S(1)} %get-tuple-element.9), channel_id=1, source_target_pairs={{0,248},{8,0},{16,8},{24,16},{32,24},{40,32},{48,40},{56,48},{64,5... | collective-permute-start | bytes 147464 | tf_op jit(solution)/shard_map/ppermute | solution.py:364
  56.6 0.0 copy-done
  56.6 0.0 copy-done.1
  56.6 2.9 %y_inner.1.partial = f32[6,16,8,256]{3,2,1,0:T(8,128)} custom-call(f32[6,16,8,256]{3,2,1,0:T(8,128)S(1)} %get-tuple-element.8.lattice, s32[16,8,256]{2,1,0:T(8,128)S(1)} %copy-done, f32[16,8,256]{2,1,0:T(8,128)S(1)} %copy-done.1), custom_call_target="tpu_custom_call" | custom-call | flops 3932160 | bytes 1572864 | tf_op jit(solution)/shard_map/y_inner/pallas_call | solution.py:327
  59.5 0.0 collective-permute-done.from_right
  59.5 0.4 collective-permute-done.1.from_left
  59.9 1.0 %y_edge.1 = f32[6,16,8,256]{3,2,1,0:T(8,128)} custom-call(f32[6,16,8,256]{3,2,1,0:T(8,128)S(1)} %get-tuple-element.8.lattice, f32[6,1,8,256]{3,2,1,0:T(8,128)S(1)} %collective-permute-done.from_right, f32[6,2,8,256]{3,2,1,0:T(8,128)S(1)} %collective-permute-done.1.from_left, s32[16,8,256]{2,1,0:T(8,128)S(1)} %copy-done, ...), custom_call_target="tpu_custom_call", output_to_operand_aliasing={{}: (5, {})} | custom-call | tf_op jit(solution)/shard_map/y_edge/pallas_call | solution.py:343
Async XLA Ops:
  44.4 12.1 %copy-start = (s32[16,8,256]{2,1,0:T(8,128)S(1)}, s32[16,8,256]{2,1,0:T(8,128)}, u32[]{:S(2)}) copy-start(s32[16,8,256]{2,1,0:T(8,128)} %y_offset.3) | copy-start | bytes 393220
  44.5 12.1 %copy-start.1 = (f32[16,8,256]{2,1,0:T(8,128)S(1)}, f32[16,8,256]{2,1,0:T(8,128)}, u32[]{:S(2)}) copy-start(f32[16,8,256]{2,1,0:T(8,128)} %y_frac.3) | copy-start | bytes 393220
  51.7 8.2 %collective-permute-start.1 = (f32[6,2,8,256]{3,2,1,0:T(8,128)S(1)}, f32[6,2,8,256]{3,2,1,0:T(8,128)S(1)}, u32[]{:S(2)}, u32[]{:S(2)}) collective-permute-start(f32[6,2,8,256]{3,2,1,0:T(8,128)S(1)} %get-tuple-element.10), channel_id=1, source_target_pairs={{0,8},{8,16},{16,24},{24,32},{32,40},{40,48},{48,56},{56,64},{64,7... | collective-permute-start | bytes 294920 | tf_op jit(solution)/shard_map/ppermute | solution.py:363
  52.0 7.5 %collective-permute-start = (f32[6,1,8,256]{3,2,1,0:T(8,128)S(1)}, f32[6,1,8,256]{3,2,1,0:T(8,128)S(1)}, u32[]{:S(2)}, u32[]{:S(2)}) collective-permute-start(f32[6,1,8,256]{3,2,1,0:T(8,128)S(1)} %get-tuple-element.9), channel_id=1, source_target_pairs={{0,248},{8,0},{16,8},{24,16},{32,24},{40,32},{48,40},{56,48},{64,5... | collective-permute-start | bytes 147464 | tf_op jit(solution)/shard_map/ppermute | solution.py:364

commit v3 on v2

--- a/solution.py
+++ b/solution.py
@@ -15,9 +15,8 @@
 SLOTS = 48
 VALUES = 8
 PEERS = 256
-CHUNK = 256
 PLANES = 8
-OWN = 8
+OWN = 7
 
 
 def kernel_weights(offset):
@@ -37,76 +36,96 @@
 
 def bucket_kernel(
     fields_h, frac_h, owner_h, slab_h, line_in_h, xcell_h, count_h, out,
-    fields, frac, owner, slab, line_in, xcell, count, sems, key_s, rank_s, place_s, upper_s, acc,
+    fields, frac, owner, slab, line_in, xcell, count, sems, key_s, rank_s, place_s, hot_s, hist_s, acc,
 ):
     moves = [
         pltpu.make_async_copy(source, goal, sems.at[number])
         for number, (source, goal) in enumerate((
-            (count_h, count), (slab_h, slab), (xcell_h, xcell), (owner_h, owner), (line_in_h, line_in), (frac_h, frac), (fields_h, fields),
+            (count_h, count), (slab_h, slab), (xcell_h, xcell), (owner_h, owner), (line_in_h, line_in), (frac_h, frac),
+            (fields_h, fields),
         ))
     ]
     for move in moves:
         move.start()
-    for move in moves:
+    for move in moves[:3]:
         move.wait()
     rows = key_s.shape[0]
     lane = lax.broadcasted_iota(jnp.int32, key_s.shape, 1)
     tile = lax.broadcasted_iota(jnp.int32, (rows, rows), 0) == lax.broadcasted_iota(jnp.int32, (rows, rows), 1)
     alive = lane < jnp.sum(jnp.where(tile, count[...], 0), axis=1, keepdims=True)
-    key = (xcell[...] >> 4) * 8 + slab[...]
-    key_s[...] = jnp.where(alive, key, -1).astype(F32)
+    key_s[...] = jnp.where(alive, (xcell[...] >> 4) * 8 + slab[...], -1).astype(F32)
+    sixteen = lax.broadcasted_iota(jnp.int32, (16, 128), 0).astype(F32)
+    one, zero = jnp.ones((), BF16), jnp.zeros((), BF16)
+
+    def wide_row(row):
+        return jnp.broadcast_to(row, (16, 128)).astype(BF16)
+
+    hist_s[...] = jnp.zeros_like(hist_s)
+    unroll = 4
+
+    def hot_step(step, carry):
+        total = hist_s[...]
+        for part in range(unroll):
+            row = step * unroll + part
+            key = wide_row(key_s[pl.ds(row, 1), :])
+            hot = jnp.concatenate(
+                [jnp.where(key == (sixteen + 16.0 * g).astype(BF16), one, zero) for g in range(PEERS // 16)], axis=0
+            )
+            hot_s[:, pl.ds(pl.multiple_of(row * 128, 128), 128)] = hot
+            total = total + hot
+        hist_s[...] = total
+        return carry
+
+    lax.fori_loop(0, rows // unroll, hot_step, 0)
+    earlier = lax.broadcasted_iota(jnp.int32, (128, 128), 0) < lax.broadcasted_iota(jnp.int32, (128, 128), 1)
+    base = jnp.dot(hist_s[...], jnp.where(earlier, 1.0, 0.0).astype(BF16), preferred_element_type=F32)
+    hist_s[...] = base.astype(BF16)
+    sub = lax.broadcasted_iota(jnp.int32, (8, 128), 0)
+    groups = rows // 8
+    keys = [key_s[g * 8:g * 8 + 8, :] for g in range(groups)]
+    above = [jnp.zeros((8, 128), F32) for _ in range(groups)]
+    for row in range(rows):
+        key = key_s[row:row + 1, :]
+        for g in range(row // 8, groups):
+            same = keys[g] == key
+            if g == row // 8:
+                same = jnp.logical_and(same, sub > row % 8)
+            above[g] = above[g] + jnp.where(same, 1.0, 0.0)
+    for g in range(groups):
+        rank_s[g * 8:g * 8 + 8, :] = above[g]
+
+    for move in moves[3:]:
+        move.wait()
     place_s[0] = (owner[...] * 8 + (line_in[...] >> 3)).astype(F32)
     place_s[1] = ((128 + (line_in[...] & 7) * 16 + (xcell[...] & 15)) * 256).astype(F32)
     place_s[2], place_s[3] = split(frac[...])
-    before = lax.broadcasted_iota(jnp.int32, (CHUNK, CHUNK), 0) < lax.broadcasted_iota(jnp.int32, (CHUNK, CHUNK), 1)
-    upper_s[...] = jnp.where(before, 1.0, 0.0).astype(BF16)
-    peer = lax.broadcasted_iota(jnp.int32, (PEERS, 128), 0).astype(F32)
-
-    def row_of(ref, row):
-        return ref[pl.ds(row, 1), :]
-
-    def hits(row):
-        return row_of(key_s, row) == peer
-
-    unroll = 4
-
-    def rank_step(step, base):
-        for part in range(unroll):
-            row = (step * unroll + part) * 2
-            hit = [hits(row + half) for half in range(2)]
-            one = jnp.concatenate([jnp.where(h, 1.0, 0.0).astype(BF16) for h in hit], axis=1)
-            earlier = jnp.dot(one, upper_s[...], preferred_element_type=F32)
-            for half in range(2):
-                seen = earlier[:, half * 128:(half + 1) * 128] + base
-                rank_s[pl.ds(row + half, 1), :] = jnp.sum(jnp.where(hit[half], seen, 0.0), axis=0, keepdims=True)
-            base = base + jnp.dot(one, jnp.ones((CHUNK, 128), BF16), preferred_element_type=F32)
-        return base
-
-    lax.fori_loop(0, rows // (2 * unroll), rank_step, jnp.zeros((PEERS, 128), F32))
-
-    slot = lax.broadcasted_iota(jnp.int32, (SLOTS, 128), 0).astype(F32)
     wide = 8
     acc[...] = jnp.zeros_like(acc)
 
-    def send_step(step, carry):
-        ones, packed = [], []
+    for step in range(rows // wide):
+        packed = []
         for part in range(wide):
             row = step * wide + part
-            ones.append(jnp.where(hits(row), 1.0, 0.0).astype(BF16))
-            here = row_of(rank_s, row) == slot
-            block = fields[:, pl.ds(pl.multiple_of(row * 128, 128), 128)]
-            high, low = split(block)
+            columns = pl.ds(row * 128, 128)
+            seen = hot_s[:, columns] * hist_s[...]
+            some = seen[0:16]
+            for g in range(1, PEERS // 16):
+                some = some + seen[g * 16:g * 16 + 16]
+            rank = jnp.sum(some.astype(F32), axis=0, keepdims=True) + rank_s[row:row + 1, :]
+            rank = wide_row(rank)
+            here = [rank == (sixteen + 16.0 * g).astype(BF16) for g in range(SLOTS // 16)]
+            high, low = split(fields[:, columns])
             highs = [high[f:f + 1] for f in range(FIELDS)]
             lows = [low[f:f + 1] for f in range(FIELDS)]
-            highs += [place_s[2, pl.ds(row, 1), :], place_s[0, pl.ds(row, 1), :]]
-            lows += [place_s[3, pl.ds(row, 1), :], place_s[1, pl.ds(row, 1), :]]
-            packed.append(jnp.concatenate([jnp.where(here, v, 0.0).astype(BF16) for v in highs + lows], axis=0))
-        acc[...] += lax.dot_general(
-            jnp.concatenate(packed, axis=1), jnp.concatenate(ones, axis=1), NT, preferred_element_type=F32
-        )
-        return carry
-
-    lax.fori_loop(0, rows // wide, send_step, 0)
+            highs += [place_s[2, row:row + 1, :], place_s[0, row:row + 1, :]]
+            lows += [place_s[3, row:row + 1, :], place_s[1, row:row + 1, :]]
+            pieces = []
+            for v in highs + lows:
+                v = wide_row(v)
+                pieces += [jnp.where(h, v, zero) for h in here]
+            packed.append(jnp.concatenate(pieces, axis=0))
+        block = hot_s[:, pl.ds(step * wide * 128, wide * 128)]
+        acc[...] += lax.dot_general(jnp.concatenate(packed, axis=1), block, NT, preferred_element_type=F32)
     half = VALUES * SLOTS
     total = acc[:half, :] + acc[half:, :]
     out[...] = jnp.swapaxes(total, 0, 1)[:, None, :]
@@ -127,18 +146,28 @@
         seen = seen + jnp.where(hit, 1.0, 0.0)
     rank = to_s[...]
     fits = rank < OWN
-    to_s[...] = jnp.where(fits, plane * OWN + rank, 9999.0)
+    to_s[...] = jnp.where(fits, plane * 8 + rank, 9999.0)
     extra = jnp.logical_and(live, jnp.logical_not(fits))
     before = lax.broadcasted_iota(jnp.int32, (SLOTS, SLOTS), 1) < lax.broadcasted_iota(jnp.int32, (SLOTS, SLOTS), 0)
     order = jnp.dot(jnp.where(before, 1.0, 0.0).astype(BF16), jnp.where(extra, 1.0, 0.0).astype(BF16), preferred_element_type=F32)
     over_s[...] = jnp.where(extra, order, -1.0)
-    rounds = jnp.max(jnp.where(extra, order, -1.0)).astype(jnp.int32) + 1
+    left = jnp.sum(jnp.maximum(seen - OWN, 0.0), axis=0, keepdims=True)
+    most = jnp.max(left, axis=1, keepdims=True)
+    few = jnp.logical_and(jnp.sum(left, axis=1, keepdims=True) <= PEERS, most <= 8)
+    rounds = jnp.max(jnp.where(few, 0.0, most)).astype(jnp.int32)
 
     low_rows = (sub + 1).astype(F32)
     high_rows = (sub + 9).astype(F32)
     edge_rows = jnp.where(sub % 4 == 0, 0, jnp.where(sub % 4 == 3, 99, 16 + sub % 4)).astype(F32)
     first = sub < 4
-    y_iota = lax.broadcasted_iota(jnp.int32, (256, PEERS), 0).astype(F32)
+    sixteen = lax.broadcasted_iota(jnp.int32, (16, PEERS), 0).astype(F32)
+    levels = [(sixteen + 16.0 * g).astype(BF16) for g in range(16)]
+
+    one, zero = jnp.ones((), BF16), jnp.zeros((), BF16)
+
+    def hot(row):
+        row = jnp.broadcast_to(row, (16, PEERS)).astype(BF16)
+        return jnp.concatenate([jnp.where(row == level, one, zero) for level in levels], axis=0)
 
     def rows_of(weights, xin, field):
         spread = []
@@ -159,36 +188,55 @@
         low = (whole - high.astype(F32)).astype(BF16)
         return jnp.concatenate([high, low], axis=0)
 
-    def planes_step(step, carry):
-        pair = 2
-        found = [[jnp.zeros((8, PEERS), F32) for _ in range(VALUES)] for _ in range(pair)]
-        goal = [subf + ((step * pair + part) * OWN).astype(F32) for part in range(pair)]
+    def gather(goals):
+        found = [[jnp.zeros((8, PEERS), F32) for _ in range(VALUES)] for _ in goals]
         for slot in range(SLOTS):
-            to = to_s[slot:slot + 1, :]
             rows = [flat_s[v * SLOTS + slot:v * SLOTS + slot + 1, :] for v in range(VALUES)]
-            for part in range(pair):
-                hit = to == goal[part]
+            for part, (numbers, goal) in enumerate(goals):
+                hit = numbers[slot:slot + 1, :] == goal
                 found[part] = [jnp.where(hit, rows[v], found[part][v]) for v in range(VALUES)]
+        return found
+
+    found = gather([(over_s, subf)])[0]
+    pieces = [split(v) for v in found]
+    stack = jnp.concatenate([p[0] for p in pieces] + [p[1] for p in pieces], axis=0).astype(BF16)
+    lanes = lax.broadcasted_iota(jnp.int32, (PEERS, PEERS), 0)
+    ahead = jnp.where(lanes < lax.broadcasted_iota(jnp.int32, (PEERS, PEERS), 1), 1.0, 0.0).astype(BF16)
+    start = jnp.dot(jnp.broadcast_to(left, (16, PEERS)).astype(BF16), ahead, preferred_element_type=F32)[0:1]
+    picked = [jnp.zeros((8, PEERS), F32) for _ in range(VALUES)]
+    for k in range(8):
+        spot = jnp.where(jnp.logical_and(left > k, few), start + k, -1.0)
+        moved = lax.dot_general(stack, hot(spot), NT, preferred_element_type=F32)
+        for v in range(VALUES):
+            value = moved[v * 8:v * 8 + 8] + moved[(VALUES + v) * 8:(VALUES + v) * 8 + 8]
+            picked[v] = jnp.where(sub == k, value, picked[v])
+    picked = [jnp.sum(v, axis=0, keepdims=True) for v in picked]
+    spot = picked[7].astype(jnp.int32)
+    few_rows = rows_of(kernel_weights(picked[6]), ((spot >> 8) & 15).astype(F32), picked[:FIELDS])
+    few_plane = (spot >> 12) & 7
+    few_y = (spot & 255).astype(F32)
+
+    pair = 2
+    for step in range(PLANES // pair):
+        found = gather([(to_s, subf + float((step * pair + part) * 8)) for part in range(pair)])
         for part in range(pair):
             spot = found[part][7].astype(jnp.int32)
+            z = step * pair + part
             for v in range(FIELDS):
-                mine_s[part, v] = found[part][v]
-            mine_s[part, 6] = ((spot >> 8) & 15).astype(F32)
-            mine_s[part, 7] = (spot & 255).astype(F32)
+                mine_s[z, v] = found[part][v]
+            mine_s[z, 6] = ((spot >> 8) & 15).astype(F32)
+            mine_s[z, 7] = (spot & 255).astype(F32)
             for number, weight in enumerate(kernel_weights(found[part][6])):
-                weight_s[part, number] = weight
-        for part in range(pair):
-            packed, ones = [], []
-            for own in range(OWN):
-                row = lambda v: mine_s[part, v, own:own + 1, :]
-                packed.append(rows_of([weight_s[part, k, own:own + 1, :] for k in range(4)], row(6), [row(f) for f in range(FIELDS)]))
-                ones.append(jnp.where(row(7) == y_iota, 1.0, 0.0).astype(BF16))
-            acc[step * pair + part] = lax.dot_general(
-                jnp.concatenate(ones, axis=1), jnp.concatenate(packed, axis=1), NT, preferred_element_type=F32
-            )
-        return carry
-
-    lax.fori_loop(0, PLANES // 2, planes_step, 0)
+                weight_s[z, number] = weight
+    for z in range(PLANES):
+        packed, ones = [few_rows], [hot(jnp.where(few_plane == z, few_y, -1.0))]
+        for own in range(OWN):
+            row = lambda v: mine_s[z, v, own:own + 1, :]
+            packed.append(rows_of([weight_s[z, k, own:own + 1, :] for k in range(4)], row(6), [row(f) for f in range(FIELDS)]))
+            ones.append(hot(row(7)))
+        acc[z] = lax.dot_general(
+            jnp.concatenate(ones, axis=1), jnp.concatenate(packed, axis=1), NT, preferred_element_type=F32
+        )
 
     def extra_step(number, carry):
         hit = over_s[...] == number.astype(F32)
@@ -200,8 +248,7 @@
         plane = (spot >> 12) & 7
         spot_y = (spot & 255).astype(F32)
         for z in range(PLANES):
-            one = jnp.where(jnp.where(plane == z, spot_y, -1.0) == y_iota, 1.0, 0.0).astype(BF16)
-            acc[z] += lax.dot_general(one, packed, NT, preferred_element_type=F32)
+            acc[z] += lax.dot_general(hot(jnp.where(plane == z, spot_y, -1.0)), packed, NT, preferred_element_type=F32)
         return carry
 
     lax.fori_loop(0, rounds, extra_step, 0)
@@ -293,7 +340,8 @@
             pltpu.VMEM((rows, 128), F32),
             pltpu.VMEM((rows, 128), F32),
             pltpu.VMEM((4, rows, 128), F32),
-            pltpu.VMEM((CHUNK, CHUNK), BF16),
+            pltpu.VMEM((PEERS, rows * 128), BF16),
+            pltpu.VMEM((PEERS, 128), BF16),
             pltpu.VMEM((2 * VALUES * SLOTS, PEERS), F32),
         ],
         compiler_params=params(56),
@@ -314,8 +362,8 @@
             pltpu.VMEM((SLOTS, PEERS), F32),
             pltpu.VMEM((SLOTS, PEERS), F32),
             pltpu.VMEM((SLOTS, PEERS), F32),
-            pltpu.VMEM((2, VALUES, 8, PEERS), F32),
-            pltpu.VMEM((2, 4, 8, PEERS), F32),
+            pltpu.VMEM((PLANES, VALUES, 8, PEERS), F32),
+            pltpu.VMEM((PLANES, 4, 8, PEERS), F32),
             pltpu.VMEM((8, 256, 256), F32),
         ],
         compiler_params=params(24),

time: 61 us -> 56.3 us (0.923)
  Pallas kernels: 21.7 us -> 17.1 us
    pallas_call x1, Pallas kernels: 10.6 us -> 7.34 us  [bucket(): pl.pallas_call(bucket_kernel, out_shape=jax.ShapeDtypeStruct((PEERS, 1, V...]
    pallas_call x1, Pallas kernels: 7.24 us -> 5.8 us  [deposit(): pl.pallas_call(deposit_kernel, out_shape=(jax.ShapeDtypeStruct((FIELDS, 1...]
where the time goes in v3:
time: 56.3 us; the launch traced here: 56.2 us
  blocking collectives  33.9 us (60%)
  Pallas kernels  17.1 us (30%)
  starting transfers between devices  4.86 us (9%)
    all_to_all x1, blocking collectives, per_device(): lax.all_to_all(outgoing, ('lines', 'slab'), split_axis=0, concat_axis=0,...  33.9 us
    pallas_call x1, Pallas kernels, bucket(): pl.pallas_call(bucket_kernel, out_shape=jax.ShapeDtypeStruct((PEERS, 1, V...  7.34 us
    pallas_call x1, Pallas kernels, deposit(): pl.pallas_call(deposit_kernel, out_shape=(jax.ShapeDtypeStruct((FIELDS, 1...  5.8 us
    ppermute x1, starting transfers between devices, per_device(): lax.ppermute(low_edge, 'lines', [(i, (i - 1) % lines) for i in range(line...  4.05 us
    pallas_call x1, Pallas kernels, y_inner(): pl.pallas_call(y_inner_kernel, out_shape=jax.ShapeDtypeStruct(lattice.sha...  2.92 us
  transfers between devices with their start and end apart: 2, of which 1 were waited for; matrix products, arithmetic and copies ran while one was open for 0% of the time, Pallas kernels for 5%

profile of v3, /device:TPU:1, one launch (start us, length us, event | category | flops | bytes accessed | tf_op | source)
XLA Modules:
  0.0 56.2 jit_solution(9455362359402379565)
XLA Ops:
  0.0 7.3 %bucket.1 = f32[256,1,384]{2,1,0:T(1,128)} custom-call(f32[6,8192]{1,0:T(8,128)} %fields_h.1, f32[64,128]{1,0:T(8,128)} %bitcast.6, s32[64,128]{1,0:T(8,128)} %bitcast.7, s32[64,128]{1,0:T(8,128)} %bitcast.8, s32[64,128]{1,0:T(8,128)} %bitcast.9, s32[64,128]{1,0:T(8,128)} %bitcast.10, s32[1,64]{1,0:T(1,128)} %bitcast.11), custom_call_target="tpu_custom_call" | custom-call | tf_op jit(solution)/shard_map/bucket/pallas_call | solution.py:327
  7.4 33.9 %all_to_all.5.arrived = f32[256,1,384]{2,1,0:T(1,128)S(1)} all-to-all(f32[256,1,384]{2,1,0:T(1,128)} %bucket.1), channel_id=1, replica_groups=mesh['lines'=32,'slab'=8] {'lines','slab'}, dimensions={0} | all-to-all | bytes 786432 | tf_op jit(solution)/shard_map/all_to_all | solution.py:409
  41.2 0.0 copy-start
  41.2 0.0 copy-start.1
  41.2 5.8 %deposit.1 = (f32[6,16,8,256]{3,2,1,0:T(8,128)S(1)}, f32[6,1,8,256]{3,2,1,0:T(8,128)S(1)}, f32[6,2,8,256]{3,2,1,0:T(8,128)S(1)}) custom-call(f32[256,1,384]{2,1,0:T(1,128)S(1)} %all_to_all.5.arrived), custom_call_target="tpu_custom_call" | custom-call | tf_op jit(solution)/shard_map/deposit/pallas_call | solution.py:353
  47.0 0.8 %collective-permute-start.1 = (f32[6,2,8,256]{3,2,1,0:T(8,128)S(1)}, f32[6,2,8,256]{3,2,1,0:T(8,128)S(1)}, u32[]{:S(2)}, u32[]{:S(2)}) collective-permute-start(f32[6,2,8,256]{3,2,1,0:T(8,128)S(1)} %get-tuple-element.10), channel_id=1, source_target_pairs={{0,8},{8,16},{16,24},{24,32},{32,40},{40,48},{48,56},{56,64},{64,7... | collective-permute-start | bytes 294920 | tf_op jit(solution)/shard_map/ppermute | solution.py:411
  47.9 4.0 %collective-permute-start = (f32[6,1,8,256]{3,2,1,0:T(8,128)S(1)}, f32[6,1,8,256]{3,2,1,0:T(8,128)S(1)}, u32[]{:S(2)}, u32[]{:S(2)}) collective-permute-start(f32[6,1,8,256]{3,2,1,0:T(8,128)S(1)} %get-tuple-element.9), channel_id=1, source_target_pairs={{0,248},{8,0},{16,8},{24,16},{32,24},{40,32},{48,40},{56,48},{64,5... | collective-permute-start | bytes 147464 | tf_op jit(solution)/shard_map/ppermute | solution.py:412
  51.9 0.0 copy-done
  51.9 0.0 copy-done.1
  51.9 2.9 %y_inner.1.partial = f32[6,16,8,256]{3,2,1,0:T(8,128)} custom-call(f32[6,16,8,256]{3,2,1,0:T(8,128)S(1)} %get-tuple-element.8.lattice, s32[16,8,256]{2,1,0:T(8,128)S(1)} %copy-done, f32[16,8,256]{2,1,0:T(8,128)S(1)} %copy-done.1), custom_call_target="tpu_custom_call" | custom-call | flops 3932160 | bytes 1572864 | tf_op jit(solution)/shard_map/y_inner/pallas_call | solution.py:375
  54.8 0.0 collective-permute-done.from_right
  54.9 0.3 collective-permute-done.1.from_left
  55.2 1.0 %y_edge.1 = f32[6,16,8,256]{3,2,1,0:T(8,128)} custom-call(f32[6,16,8,256]{3,2,1,0:T(8,128)S(1)} %get-tuple-element.8.lattice, f32[6,1,8,256]{3,2,1,0:T(8,128)S(1)} %collective-permute-done.from_right, f32[6,2,8,256]{3,2,1,0:T(8,128)S(1)} %collective-permute-done.1.from_left, s32[16,8,256]{2,1,0:T(8,128)S(1)} %copy-done, ...), custom_call_target="tpu_custom_call", output_to_operand_aliasing={{}: (5, {})} | custom-call | tf_op jit(solution)/shard_map/y_edge/pallas_call | solution.py:391
Async XLA Ops:
  41.2 10.7 %copy-start = (s32[16,8,256]{2,1,0:T(8,128)S(1)}, s32[16,8,256]{2,1,0:T(8,128)}, u32[]{:S(2)}) copy-start(s32[16,8,256]{2,1,0:T(8,128)} %y_offset.3) | copy-start | bytes 393220
  41.2 10.7 %copy-start.1 = (f32[16,8,256]{2,1,0:T(8,128)S(1)}, f32[16,8,256]{2,1,0:T(8,128)}, u32[]{:S(2)}) copy-start(f32[16,8,256]{2,1,0:T(8,128)} %y_frac.3) | copy-start | bytes 393220
  47.0 8.1 %collective-permute-start.1 = (f32[6,2,8,256]{3,2,1,0:T(8,128)S(1)}, f32[6,2,8,256]{3,2,1,0:T(8,128)S(1)}, u32[]{:S(2)}, u32[]{:S(2)}) collective-permute-start(f32[6,2,8,256]{3,2,1,0:T(8,128)S(1)} %get-tuple-element.10), channel_id=1, source_target_pairs={{0,8},{8,16},{16,24},{24,32},{32,40},{40,48},{48,56},{56,64},{64,7... | collective-permute-start | bytes 294920 | tf_op jit(solution)/shard_map/ppermute | solution.py:411
  47.9 7.0 %collective-permute-start = (f32[6,1,8,256]{3,2,1,0:T(8,128)S(1)}, f32[6,1,8,256]{3,2,1,0:T(8,128)S(1)}, u32[]{:S(2)}, u32[]{:S(2)}) collective-permute-start(f32[6,1,8,256]{3,2,1,0:T(8,128)S(1)} %get-tuple-element.9), channel_id=1, source_target_pairs={{0,248},{8,0},{16,8},{24,16},{32,24},{40,32},{48,40},{56,48},{64,5... | collective-permute-start | bytes 147464 | tf_op jit(solution)/shard_map/ppermute | solution.py:412

commit v4 on v3

--- a/solution.py
+++ b/solution.py
@@ -16,7 +16,7 @@
 VALUES = 8
 PEERS = 256
 PLANES = 8
-OWN = 7
+OWN = 6
 
 
 def kernel_weights(offset):
@@ -153,7 +153,7 @@
     over_s[...] = jnp.where(extra, order, -1.0)
     left = jnp.sum(jnp.maximum(seen - OWN, 0.0), axis=0, keepdims=True)
     most = jnp.max(left, axis=1, keepdims=True)
-    few = jnp.logical_and(jnp.sum(left, axis=1, keepdims=True) <= PEERS, most <= 8)
+    few = jnp.logical_and(jnp.sum(left, axis=1, keepdims=True) <= PEERS, most <= 16)
     rounds = jnp.max(jnp.where(few, 0.0, most)).astype(jnp.int32)
 
     low_rows = (sub + 1).astype(F32)
@@ -197,19 +197,20 @@
                 found[part] = [jnp.where(hit, rows[v], found[part][v]) for v in range(VALUES)]
         return found
 
-    found = gather([(over_s, subf)])[0]
-    pieces = [split(v) for v in found]
-    stack = jnp.concatenate([p[0] for p in pieces] + [p[1] for p in pieces], axis=0).astype(BF16)
+    stacks = []
+    for found in gather([(over_s, subf), (over_s, subf + 8.0)]):
+        pieces = [split(v) for v in found]
+        stacks.append(jnp.concatenate([p[0] for p in pieces] + [p[1] for p in pieces], axis=0).astype(BF16))
     lanes = lax.broadcasted_iota(jnp.int32, (PEERS, PEERS), 0)
     ahead = jnp.where(lanes < lax.broadcasted_iota(jnp.int32, (PEERS, PEERS), 1), 1.0, 0.0).astype(BF16)
     start = jnp.dot(jnp.broadcast_to(left, (16, PEERS)).astype(BF16), ahead, preferred_element_type=F32)[0:1]
     picked = [jnp.zeros((8, PEERS), F32) for _ in range(VALUES)]
-    for k in range(8):
+    for k in range(16):
         spot = jnp.where(jnp.logical_and(left > k, few), start + k, -1.0)
-        moved = lax.dot_general(stack, hot(spot), NT, preferred_element_type=F32)
+        moved = lax.dot_general(stacks[k // 8], hot(spot), NT, preferred_element_type=F32)
         for v in range(VALUES):
             value = moved[v * 8:v * 8 + 8] + moved[(VALUES + v) * 8:(VALUES + v) * 8 + 8]
-            picked[v] = jnp.where(sub == k, value, picked[v])
+            picked[v] = picked[v] + jnp.where(sub == k % 8, value, 0.0)
     picked = [jnp.sum(v, axis=0, keepdims=True) for v in picked]
     spot = picked[7].astype(jnp.int32)
     few_rows = rows_of(kernel_weights(picked[6]), ((spot >> 8) & 15).astype(F32), picked[:FIELDS])
@@ -288,20 +289,15 @@
 def y_inner_kernel(lattice, y_offset, y_frac, out, ready, sems):
     width = y_offset.shape[0]
 
-    def body(x, carry):
+    moves = []
+    for x in range(2, width - 1):
         factors = y_factors(y_offset[x], y_frac[x])
         for f in range(FIELDS):
             ready[x, f] = y_spread(lattice[f, x], factors)
-        pltpu.make_async_copy(ready.at[x], out.at[:, x], sems.at[x]).start()
-        return carry
-
-    lax.fori_loop(2, width - 1, body, 0)
-
-    def drain(x, carry):
-        pltpu.make_async_copy(ready.at[x], out.at[:, x], sems.at[x]).wait()
-        return carry
-
-    lax.fori_loop(2, width - 1, drain, 0)
+        moves.append(pltpu.make_async_copy(ready.at[x], out.at[:, x], sems.at[x]))
+        moves[-1].start()
+    for move in moves:
+        move.wait()
 
 
 def y_edge_kernel(lattice, from_right, from_left, y_offset, y_frac, partial, out, ready, sems):

time: 56.3 us -> 56.9 us (1.011)
  waiting for transfers between devices: 0.33 us -> 1.26 us
  Pallas kernels: 17.1 us -> 16.4 us
    ppermute x1, waiting for transfers between devices: 0.33 us -> 1.26 us  [per_device(): lax.ppermute(high_edge, 'lines', [(i, (i + 1) % lines) for i in range(lin...]
    pallas_call x1, Pallas kernels: 2.92 us -> 1.99 us  [y_inner(): pl.pallas_call(y_inner_kernel, out_shape=jax.ShapeDtypeStruct(lattice.sha...]
  transfers between devices with their start and end apart: 2 -> 2, of which waited for: 1 -> 1; matrix products, arithmetic and copies ran while one was open for 0% -> 0% of each run, Pallas kernels for 5% -> 4%
where the time goes in v4:
time: 56.9 us; the launch traced here: 56.8 us
  blocking collectives  33.9 us (60%)
  Pallas kernels  16.4 us (29%)
  starting transfers between devices  5.04 us (9%)
  waiting for transfers between devices  1.26 us (2%)
    all_to_all x1, blocking collectives, per_device(): lax.all_to_all(outgoing, ('lines', 'slab'), split_axis=0, concat_axis=0,...  33.9 us
    pallas_call x1, Pallas kernels, bucket(): pl.pallas_call(bucket_kernel, out_shape=jax.ShapeDtypeStruct((PEERS, 1, V...  7.34 us
    pallas_call x1, Pallas kernels, deposit(): pl.pallas_call(deposit_kernel, out_shape=(jax.ShapeDtypeStruct((FIELDS, 1...  6.05 us
    ppermute x1, starting transfers between devices, per_device(): lax.ppermute(low_edge, 'lines', [(i, (i - 1) % lines) for i in range(line...  4.05 us
    pallas_call x1, Pallas kernels, y_inner(): pl.pallas_call(y_inner_kernel, out_shape=jax.ShapeDtypeStruct(lattice.sha...  1.99 us
    ppermute x1, waiting for transfers between devices, per_device(): lax.ppermute(high_edge, 'lines', [(i, (i + 1) % lines) for i in range(lin...  1.26 us
  transfers between devices with their start and end apart: 2, of which 1 were waited for; matrix products, arithmetic and copies ran while one was open for 0% of the time, Pallas kernels for 4%

profile of v4, /device:TPU:1, one launch (start us, length us, event | category | flops | bytes accessed | tf_op | source)
XLA Modules:
  0.0 56.8 jit_solution(10173300806646162780)
XLA Ops:
  0.0 7.3 %bucket.1 = f32[256,1,384]{2,1,0:T(1,128)} custom-call(f32[6,8192]{1,0:T(8,128)} %fields_h.1, f32[64,128]{1,0:T(8,128)} %bitcast.6, s32[64,128]{1,0:T(8,128)} %bitcast.7, s32[64,128]{1,0:T(8,128)} %bitcast.8, s32[64,128]{1,0:T(8,128)} %bitcast.9, s32[64,128]{1,0:T(8,128)} %bitcast.10, s32[1,64]{1,0:T(1,128)} %bitcast.11), custom_call_target="tpu_custom_call" | custom-call | tf_op jit(solution)/shard_map/bucket/pallas_call | solution.py:323
  7.4 33.9 %all_to_all.5.arrived = f32[256,1,384]{2,1,0:T(1,128)S(1)} all-to-all(f32[256,1,384]{2,1,0:T(1,128)} %bucket.1), channel_id=1, replica_groups=mesh['lines'=32,'slab'=8] {'lines','slab'}, dimensions={0} | all-to-all | bytes 786432 | tf_op jit(solution)/shard_map/all_to_all | solution.py:405
  41.2 0.0 copy-start
  41.2 0.0 copy-start.1
  41.2 6.1 %deposit.1 = (f32[6,16,8,256]{3,2,1,0:T(8,128)S(1)}, f32[6,1,8,256]{3,2,1,0:T(8,128)S(1)}, f32[6,2,8,256]{3,2,1,0:T(8,128)S(1)}) custom-call(f32[256,1,384]{2,1,0:T(1,128)S(1)} %all_to_all.5.arrived), custom_call_target="tpu_custom_call" | custom-call | tf_op jit(solution)/shard_map/deposit/pallas_call | solution.py:349
  47.3 1.0 %collective-permute-start.1 = (f32[6,2,8,256]{3,2,1,0:T(8,128)S(1)}, f32[6,2,8,256]{3,2,1,0:T(8,128)S(1)}, u32[]{:S(2)}, u32[]{:S(2)}) collective-permute-start(f32[6,2,8,256]{3,2,1,0:T(8,128)S(1)} %get-tuple-element.10), channel_id=1, source_target_pairs={{0,8},{8,16},{16,24},{24,32},{32,40},{40,48},{48,56},{56,64},{64,7... | collective-permute-start | bytes 294920 | tf_op jit(solution)/shard_map/ppermute | solution.py:407
  48.3 4.0 %collective-permute-start = (f32[6,1,8,256]{3,2,1,0:T(8,128)S(1)}, f32[6,1,8,256]{3,2,1,0:T(8,128)S(1)}, u32[]{:S(2)}, u32[]{:S(2)}) collective-permute-start(f32[6,1,8,256]{3,2,1,0:T(8,128)S(1)} %get-tuple-element.9), channel_id=1, source_target_pairs={{0,248},{8,0},{16,8},{24,16},{32,24},{40,32},{48,40},{56,48},{64,5... | collective-permute-start | bytes 147464 | tf_op jit(solution)/shard_map/ppermute | solution.py:408
  52.3 0.0 copy-done
  52.3 0.0 copy-done.1
  52.3 2.0 %y_inner.1.partial = f32[6,16,8,256]{3,2,1,0:T(8,128)} custom-call(f32[6,16,8,256]{3,2,1,0:T(8,128)S(1)} %get-tuple-element.8.lattice, s32[16,8,256]{2,1,0:T(8,128)S(1)} %copy-done, f32[16,8,256]{2,1,0:T(8,128)S(1)} %copy-done.1), custom_call_target="tpu_custom_call" | custom-call | flops 3932160 | bytes 1572864 | tf_op jit(solution)/shard_map/y_inner/pallas_call | solution.py:371
  54.3 0.0 collective-permute-done.from_right
  54.3 1.3 %collective-permute-done.1.from_left = f32[6,2,8,256]{3,2,1,0:T(8,128)S(1)} collective-permute-done((f32[6,2,8,256]{3,2,1,0:T(8,128)S(1)}, f32[6,2,8,256]{3,2,1,0:T(8,128)S(1)}, u32[]{:S(2)}, u32[]{:S(2)}) %collective-permute-start.1) | collective-permute-done | bytes 98336 | tf_op jit(solution)/shard_map/ppermute | solution.py:407
  55.6 1.0 %y_edge.1 = f32[6,16,8,256]{3,2,1,0:T(8,128)} custom-call(f32[6,16,8,256]{3,2,1,0:T(8,128)S(1)} %get-tuple-element.8.lattice, f32[6,1,8,256]{3,2,1,0:T(8,128)S(1)} %collective-permute-done.from_right, f32[6,2,8,256]{3,2,1,0:T(8,128)S(1)} %collective-permute-done.1.from_left, s32[16,8,256]{2,1,0:T(8,128)S(1)} %copy-done, ...), custom_call_target="tpu_custom_call", output_to_operand_aliasing={{}: (5, {})} | custom-call | tf_op jit(solution)/shard_map/y_edge/pallas_call | solution.py:387
Async XLA Ops:
  41.2 11.1 %copy-start = (s32[16,8,256]{2,1,0:T(8,128)S(1)}, s32[16,8,256]{2,1,0:T(8,128)}, u32[]{:S(2)}) copy-start(s32[16,8,256]{2,1,0:T(8,128)} %y_offset.3) | copy-start | bytes 393220
  41.2 11.1 %copy-start.1 = (f32[16,8,256]{2,1,0:T(8,128)S(1)}, f32[16,8,256]{2,1,0:T(8,128)}, u32[]{:S(2)}) copy-start(f32[16,8,256]{2,1,0:T(8,128)} %y_frac.3) | copy-start | bytes 393220
  47.3 8.3 %collective-permute-start.1 = (f32[6,2,8,256]{3,2,1,0:T(8,128)S(1)}, f32[6,2,8,256]{3,2,1,0:T(8,128)S(1)}, u32[]{:S(2)}, u32[]{:S(2)}) collective-permute-start(f32[6,2,8,256]{3,2,1,0:T(8,128)S(1)} %get-tuple-element.10), channel_id=1, source_target_pairs={{0,8},{8,16},{16,24},{24,32},{32,40},{40,48},{48,56},{56,64},{64,7... | collective-permute-start | bytes 294920 | tf_op jit(solution)/shard_map/ppermute | solution.py:407
  48.3 6.0 %collective-permute-start = (f32[6,1,8,256]{3,2,1,0:T(8,128)S(1)}, f32[6,1,8,256]{3,2,1,0:T(8,128)S(1)}, u32[]{:S(2)}, u32[]{:S(2)}) collective-permute-start(f32[6,1,8,256]{3,2,1,0:T(8,128)S(1)} %get-tuple-element.9), channel_id=1, source_target_pairs={{0,248},{8,0},{16,8},{24,16},{32,24},{40,32},{48,40},{56,48},{64,5... | collective-permute-start | bytes 147464 | tf_op jit(solution)/shard_map/ppermute | solution.py:408

commit v5 on v4

--- a/solution.py
+++ b/solution.py
@@ -60,25 +60,16 @@
     def wide_row(row):
         return jnp.broadcast_to(row, (16, 128)).astype(BF16)
 
-    hist_s[...] = jnp.zeros_like(hist_s)
-    unroll = 4
-
-    def hot_step(step, carry):
-        total = hist_s[...]
-        for part in range(unroll):
-            row = step * unroll + part
-            key = wide_row(key_s[pl.ds(row, 1), :])
-            hot = jnp.concatenate(
-                [jnp.where(key == (sixteen + 16.0 * g).astype(BF16), one, zero) for g in range(PEERS // 16)], axis=0
-            )
-            hot_s[:, pl.ds(pl.multiple_of(row * 128, 128), 128)] = hot
-            total = total + hot
-        hist_s[...] = total
-        return carry
-
-    lax.fori_loop(0, rows // unroll, hot_step, 0)
+    total = jnp.zeros((PEERS, 128), BF16)
+    for row in range(rows):
+        key = wide_row(key_s[row:row + 1, :])
+        hot = jnp.concatenate(
+            [jnp.where(key == (sixteen + 16.0 * g).astype(BF16), one, zero) for g in range(PEERS // 16)], axis=0
+        )
+        hot_s[:, row * 128:row * 128 + 128] = hot
+        total = total + hot
     earlier = lax.broadcasted_iota(jnp.int32, (128, 128), 0) < lax.broadcasted_iota(jnp.int32, (128, 128), 1)
-    base = jnp.dot(hist_s[...], jnp.where(earlier, 1.0, 0.0).astype(BF16), preferred_element_type=F32)
+    base = jnp.dot(total, jnp.where(earlier, 1.0, 0.0).astype(BF16), preferred_element_type=F32)
     hist_s[...] = base.astype(BF16)
     sub = lax.broadcasted_iota(jnp.int32, (8, 128), 0)
     groups = rows // 8
@@ -253,6 +244,7 @@
         return carry
 
     lax.fori_loop(0, rounds, extra_step, 0)
+    low_edge[:, 1] = jnp.zeros((FIELDS,) + low_edge.shape[2:], F32)
     for z in range(PLANES):
         nodes = jnp.swapaxes(acc[z, :, :128] + acc[z, :, 128:], 0, 1)
         for f in range(FIELDS):
@@ -350,7 +342,7 @@
         deposit_kernel,
         out_shape=(
             jax.ShapeDtypeStruct((FIELDS, 16, 8, 256), F32),
-            jax.ShapeDtypeStruct((FIELDS, 1, 8, 256), F32),
+            jax.ShapeDtypeStruct((FIELDS, 2, 8, 256), F32),
             jax.ShapeDtypeStruct((FIELDS, 2, 8, 256), F32),
         ),
         scratch_shapes=[

time: 56.9 us -> 55.7 us (0.979)
  starting transfers between devices: 5.04 us -> 1.54 us
  waiting for transfers between devices: 1.26 us -> 3.94 us
    ppermute x1, starting transfers between devices: 4.05 us -> 0.7 us  [per_device(): lax.ppermute(low_edge, 'lines', [(i, (i - 1) % lines) for i in range(line...]
    ppermute x1, waiting for transfers between devices: 1.26 us -> 2.67 us  [per_device(): lax.ppermute(high_edge, 'lines', [(i, (i + 1) % lines) for i in range(lin...]
    ppermute x1, waiting for transfers between devices: 0.01 us -> 1.27 us  [per_device(): lax.ppermute(low_edge, 'lines', [(i, (i - 1) % lines) for i in range(line...]
  transfers between devices with their start and end apart: 2 -> 2, of which waited for: 1 -> 2; matrix products, arithmetic and copies ran while one was open for 0% -> 0% of each run, Pallas kernels for 4% -> 4%
where the time goes in v5:
time: 55.7 us; the launch traced here: 55.6 us
  blocking collectives  33.9 us (61%)
  Pallas kernels  16 us (29%)
  waiting for transfers between devices  3.94 us (7%)
  starting transfers between devices  1.54 us (3%)
    all_to_all x1, blocking collectives, per_device(): lax.all_to_all(outgoing, ('lines', 'slab'), split_axis=0, concat_axis=0,...  33.9 us
    pallas_call x1, Pallas kernels, bucket(): pl.pallas_call(bucket_kernel, out_shape=jax.ShapeDtypeStruct((PEERS, 1, V...  6.79 us
    pallas_call x1, Pallas kernels, deposit(): pl.pallas_call(deposit_kernel, out_shape=(jax.ShapeDtypeStruct((FIELDS, 1...  6.23 us
    ppermute x1, waiting for transfers between devices, per_device(): lax.ppermute(high_edge, 'lines', [(i, (i + 1) % lines) for i in range(lin...  2.67 us
    pallas_call x1, Pallas kernels, y_inner(): pl.pallas_call(y_inner_kernel, out_shape=jax.ShapeDtypeStruct(lattice.sha...  1.99 us
    ppermute x1, waiting for transfers between devices, per_device(): lax.ppermute(low_edge, 'lines', [(i, (i - 1) % lines) for i in range(line...  1.27 us
  transfers between devices with their start and end apart: 2, of which 2 were waited for; matrix products, arithmetic and copies ran while one was open for 0% of the time, Pallas kernels for 4%

profile of v5, /device:TPU:1, one launch (start us, length us, event | category | flops | bytes accessed | tf_op | source)
XLA Modules:
  0.0 55.6 jit_solution(12786855198613372933)
XLA Ops:
  0.0 6.8 %bucket.1 = f32[256,1,384]{2,1,0:T(1,128)} custom-call(f32[6,8192]{1,0:T(8,128)} %fields_h.1, f32[64,128]{1,0:T(8,128)} %bitcast.6, s32[64,128]{1,0:T(8,128)} %bitcast.7, s32[64,128]{1,0:T(8,128)} %bitcast.8, s32[64,128]{1,0:T(8,128)} %bitcast.9, s32[64,128]{1,0:T(8,128)} %bitcast.10, s32[1,64]{1,0:T(1,128)} %bitcast.11), custom_call_target="tpu_custom_call" | custom-call | tf_op jit(solution)/shard_map/bucket/pallas_call | solution.py:315
  6.8 33.9 %all_to_all.5.arrived = f32[256,1,384]{2,1,0:T(1,128)S(1)} all-to-all(f32[256,1,384]{2,1,0:T(1,128)} %bucket.1), channel_id=1, replica_groups=mesh['lines'=32,'slab'=8] {'lines','slab'}, dimensions={0} | all-to-all | bytes 786432 | tf_op jit(solution)/shard_map/all_to_all | solution.py:397
  40.7 0.0 copy-start
  40.7 0.0 copy-start.1
  40.7 6.2 %deposit.1 = (f32[6,16,8,256]{3,2,1,0:T(8,128)S(1)}, f32[6,2,8,256]{3,2,1,0:T(8,128)S(1)}, f32[6,2,8,256]{3,2,1,0:T(8,128)S(1)}) custom-call(f32[256,1,384]{2,1,0:T(1,128)S(1)} %all_to_all.5.arrived), custom_call_target="tpu_custom_call" | custom-call | tf_op jit(solution)/shard_map/deposit/pallas_call | solution.py:341
  46.9 0.7 %collective-permute-start = (f32[6,2,8,256]{3,2,1,0:T(8,128)S(1)}, f32[6,2,8,256]{3,2,1,0:T(8,128)S(1)}, u32[]{:S(2)}, u32[]{:S(2)}) collective-permute-start(f32[6,2,8,256]{3,2,1,0:T(8,128)S(1)} %get-tuple-element.9), channel_id=1, source_target_pairs={{0,248},{8,0},{16,8},{24,16},{32,24},{40,32},{48,40},{56,48},{64,5... | collective-permute-start | bytes 294920 | tf_op jit(solution)/shard_map/ppermute | solution.py:400
  47.6 0.8 %collective-permute-start.1 = (f32[6,2,8,256]{3,2,1,0:T(8,128)S(1)}, f32[6,2,8,256]{3,2,1,0:T(8,128)S(1)}, u32[]{:S(2)}, u32[]{:S(2)}) collective-permute-start(f32[6,2,8,256]{3,2,1,0:T(8,128)S(1)} %get-tuple-element.10), channel_id=1, source_target_pairs={{0,8},{8,16},{16,24},{24,32},{32,40},{40,48},{48,56},{56,64},{64,7... | collective-permute-start | bytes 294920 | tf_op jit(solution)/shard_map/ppermute | solution.py:399
  48.5 0.0 copy-done
  48.5 0.0 copy-done.1
  48.5 2.0 %y_inner.1.partial = f32[6,16,8,256]{3,2,1,0:T(8,128)} custom-call(f32[6,16,8,256]{3,2,1,0:T(8,128)S(1)} %get-tuple-element.8.lattice, s32[16,8,256]{2,1,0:T(8,128)S(1)} %copy-done, f32[16,8,256]{2,1,0:T(8,128)S(1)} %copy-done.1), custom_call_target="tpu_custom_call" | custom-call | flops 3932160 | bytes 1572864 | tf_op jit(solution)/shard_map/y_inner/pallas_call | solution.py:363
  50.5 1.3 %collective-permute-done.from_right = f32[6,2,8,256]{3,2,1,0:T(8,128)S(1)} collective-permute-done((f32[6,2,8,256]{3,2,1,0:T(8,128)S(1)}, f32[6,2,8,256]{3,2,1,0:T(8,128)S(1)}, u32[]{:S(2)}, u32[]{:S(2)}) %collective-permute-start) | collective-permute-done | bytes 98336 | tf_op jit(solution)/shard_map/ppermute | solution.py:400
  51.7 2.7 %collective-permute-done.1.from_left = f32[6,2,8,256]{3,2,1,0:T(8,128)S(1)} collective-permute-done((f32[6,2,8,256]{3,2,1,0:T(8,128)S(1)}, f32[6,2,8,256]{3,2,1,0:T(8,128)S(1)}, u32[]{:S(2)}, u32[]{:S(2)}) %collective-permute-start.1) | collective-permute-done | bytes 98336 | tf_op jit(solution)/shard_map/ppermute | solution.py:399
  54.4 1.0 %y_edge.1 = f32[6,16,8,256]{3,2,1,0:T(8,128)} custom-call(f32[6,16,8,256]{3,2,1,0:T(8,128)S(1)} %get-tuple-element.8.lattice, f32[6,2,8,256]{3,2,1,0:T(8,128)S(1)} %collective-permute-done.from_right, f32[6,2,8,256]{3,2,1,0:T(8,128)S(1)} %collective-permute-done.1.from_left, s32[16,8,256]{2,1,0:T(8,128)S(1)} %copy-done, ...), custom_call_target="tpu_custom_call", output_to_operand_aliasing={{}: (5, {})} | custom-call | tf_op jit(solution)/shard_map/y_edge/pallas_call | solution.py:379
Async XLA Ops:
  40.7 7.8 %copy-start = (s32[16,8,256]{2,1,0:T(8,128)S(1)}, s32[16,8,256]{2,1,0:T(8,128)}, u32[]{:S(2)}) copy-start(s32[16,8,256]{2,1,0:T(8,128)} %y_offset.3) | copy-start | bytes 393220
  40.7 7.8 %copy-start.1 = (f32[16,8,256]{2,1,0:T(8,128)S(1)}, f32[16,8,256]{2,1,0:T(8,128)}, u32[]{:S(2)}) copy-start(f32[16,8,256]{2,1,0:T(8,128)} %y_frac.3) | copy-start | bytes 393220
  46.9 4.8 %collective-permute-start = (f32[6,2,8,256]{3,2,1,0:T(8,128)S(1)}, f32[6,2,8,256]{3,2,1,0:T(8,128)S(1)}, u32[]{:S(2)}, u32[]{:S(2)}) collective-permute-start(f32[6,2,8,256]{3,2,1,0:T(8,128)S(1)} %get-tuple-element.9), channel_id=1, source_target_pairs={{0,248},{8,0},{16,8},{24,16},{32,24},{40,32},{48,40},{56,48},{64,5... | collective-permute-start | bytes 294920 | tf_op jit(solution)/shard_map/ppermute | solution.py:400
  47.6 6.8 %collective-permute-start.1 = (f32[6,2,8,256]{3,2,1,0:T(8,128)S(1)}, f32[6,2,8,256]{3,2,1,0:T(8,128)S(1)}, u32[]{:S(2)}, u32[]{:S(2)}) collective-permute-start(f32[6,2,8,256]{3,2,1,0:T(8,128)S(1)} %get-tuple-element.10), channel_id=1, source_target_pairs={{0,8},{8,16},{16,24},{24,32},{32,40},{40,48},{48,56},{56,64},{64,7... | collective-permute-start | bytes 294920 | tf_op jit(solution)/shard_map/ppermute | solution.py:399

commit v6 on v5

--- a/solution.py
+++ b/solution.py
@@ -144,8 +144,10 @@
     over_s[...] = jnp.where(extra, order, -1.0)
     left = jnp.sum(jnp.maximum(seen - OWN, 0.0), axis=0, keepdims=True)
     most = jnp.max(left, axis=1, keepdims=True)
-    few = jnp.logical_and(jnp.sum(left, axis=1, keepdims=True) <= PEERS, most <= 16)
-    rounds = jnp.max(jnp.where(few, 0.0, most)).astype(jnp.int32)
+    tiled = jnp.minimum(left, 16.0)
+    few = jnp.sum(tiled, axis=1, keepdims=True) <= PEERS
+    first_round = jnp.max(jnp.where(few, 16.0, 0.0)).astype(jnp.int32)
+    last_round = jnp.max(most).astype(jnp.int32)
 
     low_rows = (sub + 1).astype(F32)
     high_rows = (sub + 9).astype(F32)
@@ -194,7 +196,7 @@
         stacks.append(jnp.concatenate([p[0] for p in pieces] + [p[1] for p in pieces], axis=0).astype(BF16))
     lanes = lax.broadcasted_iota(jnp.int32, (PEERS, PEERS), 0)
     ahead = jnp.where(lanes < lax.broadcasted_iota(jnp.int32, (PEERS, PEERS), 1), 1.0, 0.0).astype(BF16)
-    start = jnp.dot(jnp.broadcast_to(left, (16, PEERS)).astype(BF16), ahead, preferred_element_type=F32)[0:1]
+    start = jnp.dot(jnp.broadcast_to(tiled, (16, PEERS)).astype(BF16), ahead, preferred_element_type=F32)[0:1]
     picked = [jnp.zeros((8, PEERS), F32) for _ in range(VALUES)]
     for k in range(16):
         spot = jnp.where(jnp.logical_and(left > k, few), start + k, -1.0)
@@ -243,7 +245,7 @@
             acc[z] += lax.dot_general(hot(jnp.where(plane == z, spot_y, -1.0)), packed, NT, preferred_element_type=F32)
         return carry
 
-    lax.fori_loop(0, rounds, extra_step, 0)
+    lax.fori_loop(first_round, last_round, extra_step, 0)
     low_edge[:, 1] = jnp.zeros((FIELDS,) + low_edge.shape[2:], F32)
     for z in range(PLANES):
         nodes = jnp.swapaxes(acc[z, :, :128] + acc[z, :, 128:], 0, 1)

time: 55.7 us -> 55.6 us (level)
  no operation moved by 1% of the time
where the time goes in v6:
time: 55.6 us; the launch traced here: 55.4 us
  blocking collectives  33.9 us (61%)
  Pallas kernels  15.9 us (29%)
  waiting for transfers between devices  3.94 us (7%)
  starting transfers between devices  1.54 us (3%)
    all_to_all x1, blocking collectives, per_device(): lax.all_to_all(outgoing, ('lines', 'slab'), split_axis=0, concat_axis=0,...  33.9 us
    pallas_call x1, Pallas kernels, bucket(): pl.pallas_call(bucket_kernel, out_shape=jax.ShapeDtypeStruct((PEERS, 1, V...  6.79 us
    pallas_call x1, Pallas kernels, deposit(): pl.pallas_call(deposit_kernel, out_shape=(jax.ShapeDtypeStruct((FIELDS, 1...  6.1 us
    ppermute x1, waiting for transfers between devices, per_device(): lax.ppermute(high_edge, 'lines', [(i, (i + 1) % lines) for i in range(lin...  2.66 us
    pallas_call x1, Pallas kernels, y_inner(): pl.pallas_call(y_inner_kernel, out_shape=jax.ShapeDtypeStruct(lattice.sha...  1.99 us
    ppermute x1, waiting for transfers between devices, per_device(): lax.ppermute(low_edge, 'lines', [(i, (i - 1) % lines) for i in range(line...  1.27 us
  transfers between devices with their start and end apart: 2, of which 2 were waited for; matrix products, arithmetic and copies ran while one was open for 0% of the time, Pallas kernels for 4%

profile of v6, /device:TPU:1, one launch (start us, length us, event | category | flops | bytes accessed | tf_op | source)
XLA Modules:
  0.0 55.4 jit_solution(544342062026924614)
XLA Ops:
  0.0 6.8 %bucket.1 = f32[256,1,384]{2,1,0:T(1,128)} custom-call(f32[6,8192]{1,0:T(8,128)} %fields_h.1, f32[64,128]{1,0:T(8,128)} %bitcast.6, s32[64,128]{1,0:T(8,128)} %bitcast.7, s32[64,128]{1,0:T(8,128)} %bitcast.8, s32[64,128]{1,0:T(8,128)} %bitcast.9, s32[64,128]{1,0:T(8,128)} %bitcast.10, s32[1,64]{1,0:T(1,128)} %bitcast.11), custom_call_target="tpu_custom_call" | custom-call | tf_op jit(solution)/shard_map/bucket/pallas_call | solution.py:317
  6.8 33.9 %all_to_all.5.arrived = f32[256,1,384]{2,1,0:T(1,128)S(1)} all-to-all(f32[256,1,384]{2,1,0:T(1,128)} %bucket.1), channel_id=1, replica_groups=mesh['lines'=32,'slab'=8] {'lines','slab'}, dimensions={0} | all-to-all | bytes 786432 | tf_op jit(solution)/shard_map/all_to_all | solution.py:399
  40.7 0.0 copy-start
  40.7 0.0 copy-start.1
  40.7 6.1 %deposit.1 = (f32[6,16,8,256]{3,2,1,0:T(8,128)S(1)}, f32[6,2,8,256]{3,2,1,0:T(8,128)S(1)}, f32[6,2,8,256]{3,2,1,0:T(8,128)S(1)}) custom-call(f32[256,1,384]{2,1,0:T(1,128)S(1)} %all_to_all.5.arrived), custom_call_target="tpu_custom_call" | custom-call | tf_op jit(solution)/shard_map/deposit/pallas_call | solution.py:343
  46.8 0.7 %collective-permute-start = (f32[6,2,8,256]{3,2,1,0:T(8,128)S(1)}, f32[6,2,8,256]{3,2,1,0:T(8,128)S(1)}, u32[]{:S(2)}, u32[]{:S(2)}) collective-permute-start(f32[6,2,8,256]{3,2,1,0:T(8,128)S(1)} %get-tuple-element.9), channel_id=1, source_target_pairs={{0,248},{8,0},{16,8},{24,16},{32,24},{40,32},{48,40},{56,48},{64,5... | collective-permute-start | bytes 294920 | tf_op jit(solution)/shard_map/ppermute | solution.py:402
  47.5 0.8 %collective-permute-start.1 = (f32[6,2,8,256]{3,2,1,0:T(8,128)S(1)}, f32[6,2,8,256]{3,2,1,0:T(8,128)S(1)}, u32[]{:S(2)}, u32[]{:S(2)}) collective-permute-start(f32[6,2,8,256]{3,2,1,0:T(8,128)S(1)} %get-tuple-element.10), channel_id=1, source_target_pairs={{0,8},{8,16},{16,24},{24,32},{32,40},{40,48},{48,56},{56,64},{64,7... | collective-permute-start | bytes 294920 | tf_op jit(solution)/shard_map/ppermute | solution.py:401
  48.3 0.0 copy-done
  48.3 0.0 copy-done.1
  48.3 2.0 %y_inner.1.partial = f32[6,16,8,256]{3,2,1,0:T(8,128)} custom-call(f32[6,16,8,256]{3,2,1,0:T(8,128)S(1)} %get-tuple-element.8.lattice, s32[16,8,256]{2,1,0:T(8,128)S(1)} %copy-done, f32[16,8,256]{2,1,0:T(8,128)S(1)} %copy-done.1), custom_call_target="tpu_custom_call" | custom-call | flops 3932160 | bytes 1572864 | tf_op jit(solution)/shard_map/y_inner/pallas_call | solution.py:365
  50.3 1.3 %collective-permute-done.from_right = f32[6,2,8,256]{3,2,1,0:T(8,128)S(1)} collective-permute-done((f32[6,2,8,256]{3,2,1,0:T(8,128)S(1)}, f32[6,2,8,256]{3,2,1,0:T(8,128)S(1)}, u32[]{:S(2)}, u32[]{:S(2)}) %collective-permute-start) | collective-permute-done | bytes 98336 | tf_op jit(solution)/shard_map/ppermute | solution.py:402
  51.6 2.7 %collective-permute-done.1.from_left = f32[6,2,8,256]{3,2,1,0:T(8,128)S(1)} collective-permute-done((f32[6,2,8,256]{3,2,1,0:T(8,128)S(1)}, f32[6,2,8,256]{3,2,1,0:T(8,128)S(1)}, u32[]{:S(2)}, u32[]{:S(2)}) %collective-permute-start.1) | collective-permute-done | bytes 98336 | tf_op jit(solution)/shard_map/ppermute | solution.py:401
  54.3 1.0 %y_edge.1 = f32[6,16,8,256]{3,2,1,0:T(8,128)} custom-call(f32[6,16,8,256]{3,2,1,0:T(8,128)S(1)} %get-tuple-element.8.lattice, f32[6,2,8,256]{3,2,1,0:T(8,128)S(1)} %collective-permute-done.from_right, f32[6,2,8,256]{3,2,1,0:T(8,128)S(1)} %collective-permute-done.1.from_left, s32[16,8,256]{2,1,0:T(8,128)S(1)} %copy-done, ...), custom_call_target="tpu_custom_call", output_to_operand_aliasing={{}: (5, {})} | custom-call | tf_op jit(solution)/shard_map/y_edge/pallas_call | solution.py:381
Async XLA Ops:
  40.7 7.7 %copy-start = (s32[16,8,256]{2,1,0:T(8,128)S(1)}, s32[16,8,256]{2,1,0:T(8,128)}, u32[]{:S(2)}) copy-start(s32[16,8,256]{2,1,0:T(8,128)} %y_offset.3) | copy-start | bytes 393220
  40.7 7.7 %copy-start.1 = (f32[16,8,256]{2,1,0:T(8,128)S(1)}, f32[16,8,256]{2,1,0:T(8,128)}, u32[]{:S(2)}) copy-start(f32[16,8,256]{2,1,0:T(8,128)} %y_frac.3) | copy-start | bytes 393220
  46.8 4.8 %collective-permute-start = (f32[6,2,8,256]{3,2,1,0:T(8,128)S(1)}, f32[6,2,8,256]{3,2,1,0:T(8,128)S(1)}, u32[]{:S(2)}, u32[]{:S(2)}) collective-permute-start(f32[6,2,8,256]{3,2,1,0:T(8,128)S(1)} %get-tuple-element.9), channel_id=1, source_target_pairs={{0,248},{8,0},{16,8},{24,16},{32,24},{40,32},{48,40},{56,48},{64,5... | collective-permute-start | bytes 294920 | tf_op jit(solution)/shard_map/ppermute | solution.py:402
  47.5 6.8 %collective-permute-start.1 = (f32[6,2,8,256]{3,2,1,0:T(8,128)S(1)}, f32[6,2,8,256]{3,2,1,0:T(8,128)S(1)}, u32[]{:S(2)}, u32[]{:S(2)}) collective-permute-start(f32[6,2,8,256]{3,2,1,0:T(8,128)S(1)} %get-tuple-element.10), channel_id=1, source_target_pairs={{0,8},{8,16},{16,24},{24,32},{32,40},{40,48},{48,56},{56,64},{64,7... | collective-permute-start | bytes 294920 | tf_op jit(solution)/shard_map/ppermute | solution.py:401

commit v7 on v6

--- a/solution.py
+++ b/solution.py
@@ -90,7 +90,7 @@
     place_s[0] = (owner[...] * 8 + (line_in[...] >> 3)).astype(F32)
     place_s[1] = ((128 + (line_in[...] & 7) * 16 + (xcell[...] & 15)) * 256).astype(F32)
     place_s[2], place_s[3] = split(frac[...])
-    wide = 8
+    wide = 16
     acc[...] = jnp.zeros_like(acc)
 
     for step in range(rows // wide):
@@ -164,10 +164,10 @@
 
     def rows_of(weights, xin, field):
         spread = []
-        for nodes in (low_rows, high_rows, edge_rows):
+        for nodes, reach in ((low_rows, range(4)), (high_rows, range(4)), (edge_rows, (0, 2, 3))):
             apart = nodes - xin
             value = jnp.zeros((8, PEERS), F32)
-            for k in range(4):
+            for k in reach:
                 value = jnp.where(apart == float(k), weights[k], value)
             spread.append(value)
         groups = []
@@ -210,7 +210,7 @@
     few_plane = (spot >> 12) & 7
     few_y = (spot & 255).astype(F32)
 
-    pair = 2
+    pair = 1
     for step in range(PLANES // pair):
         found = gather([(to_s, subf + float((step * pair + part) * 8)) for part in range(pair)])
         for part in range(pair):

time: 55.6 us -> 55.5 us (level)
  no operation moved by 1% of the time
where the time goes in v7:
time: 55.5 us; the launch traced here: 55.4 us
  blocking collectives  33.9 us (61%)
  Pallas kernels  15.8 us (28%)
  waiting for transfers between devices  3.94 us (7%)
  starting transfers between devices  1.54 us (3%)
    all_to_all x1, blocking collectives, per_device(): lax.all_to_all(outgoing, ('lines', 'slab'), split_axis=0, concat_axis=0,...  33.9 us
    pallas_call x1, Pallas kernels, bucket(): pl.pallas_call(bucket_kernel, out_shape=jax.ShapeDtypeStruct((PEERS, 1, V...  6.79 us
    pallas_call x1, Pallas kernels, deposit(): pl.pallas_call(deposit_kernel, out_shape=(jax.ShapeDtypeStruct((FIELDS, 1...  6.05 us
    ppermute x1, waiting for transfers between devices, per_device(): lax.ppermute(high_edge, 'lines', [(i, (i + 1) % lines) for i in range(lin...  2.68 us
    pallas_call x1, Pallas kernels, y_inner(): pl.pallas_call(y_inner_kernel, out_shape=jax.ShapeDtypeStruct(lattice.sha...  1.99 us
    ppermute x1, waiting for transfers between devices, per_device(): lax.ppermute(low_edge, 'lines', [(i, (i - 1) % lines) for i in range(line...  1.26 us
  transfers between devices with their start and end apart: 2, of which 2 were waited for; matrix products, arithmetic and copies ran while one was open for 0% of the time, Pallas kernels for 4%

profile of v7, /device:TPU:1, one launch (start us, length us, event | category | flops | bytes accessed | tf_op | source)
XLA Modules:
  0.0 55.4 jit_solution(17476213653623084903)
XLA Ops:
  0.0 6.8 %bucket.1 = f32[256,1,384]{2,1,0:T(1,128)} custom-call(f32[6,8192]{1,0:T(8,128)} %fields_h.1, f32[64,128]{1,0:T(8,128)} %bitcast.6, s32[64,128]{1,0:T(8,128)} %bitcast.7, s32[64,128]{1,0:T(8,128)} %bitcast.8, s32[64,128]{1,0:T(8,128)} %bitcast.9, s32[64,128]{1,0:T(8,128)} %bitcast.10, s32[1,64]{1,0:T(1,128)} %bitcast.11), custom_call_target="tpu_custom_call" | custom-call | tf_op jit(solution)/shard_map/bucket/pallas_call | solution.py:317
  6.8 33.9 %all_to_all.5.arrived = f32[256,1,384]{2,1,0:T(1,128)S(1)} all-to-all(f32[256,1,384]{2,1,0:T(1,128)} %bucket.1), channel_id=1, replica_groups=mesh['lines'=32,'slab'=8] {'lines','slab'}, dimensions={0} | all-to-all | bytes 786432 | tf_op jit(solution)/shard_map/all_to_all | solution.py:399
  40.7 0.0 copy-start
  40.7 0.0 copy-start.1
  40.7 6.1 %deposit.1 = (f32[6,16,8,256]{3,2,1,0:T(8,128)S(1)}, f32[6,2,8,256]{3,2,1,0:T(8,128)S(1)}, f32[6,2,8,256]{3,2,1,0:T(8,128)S(1)}) custom-call(f32[256,1,384]{2,1,0:T(1,128)S(1)} %all_to_all.5.arrived), custom_call_target="tpu_custom_call" | custom-call | tf_op jit(solution)/shard_map/deposit/pallas_call | solution.py:343
  46.7 0.7 %collective-permute-start = (f32[6,2,8,256]{3,2,1,0:T(8,128)S(1)}, f32[6,2,8,256]{3,2,1,0:T(8,128)S(1)}, u32[]{:S(2)}, u32[]{:S(2)}) collective-permute-start(f32[6,2,8,256]{3,2,1,0:T(8,128)S(1)} %get-tuple-element.9), channel_id=1, source_target_pairs={{0,248},{8,0},{16,8},{24,16},{32,24},{40,32},{48,40},{56,48},{64,5... | collective-permute-start | bytes 294920 | tf_op jit(solution)/shard_map/ppermute | solution.py:402
  47.4 0.8 %collective-permute-start.1 = (f32[6,2,8,256]{3,2,1,0:T(8,128)S(1)}, f32[6,2,8,256]{3,2,1,0:T(8,128)S(1)}, u32[]{:S(2)}, u32[]{:S(2)}) collective-permute-start(f32[6,2,8,256]{3,2,1,0:T(8,128)S(1)} %get-tuple-element.10), channel_id=1, source_target_pairs={{0,8},{8,16},{16,24},{24,32},{32,40},{40,48},{48,56},{56,64},{64,7... | collective-permute-start | bytes 294920 | tf_op jit(solution)/shard_map/ppermute | solution.py:401
  48.3 0.0 copy-done
  48.3 0.0 copy-done.1
  48.3 2.0 %y_inner.1.partial = f32[6,16,8,256]{3,2,1,0:T(8,128)} custom-call(f32[6,16,8,256]{3,2,1,0:T(8,128)S(1)} %get-tuple-element.8.lattice, s32[16,8,256]{2,1,0:T(8,128)S(1)} %copy-done, f32[16,8,256]{2,1,0:T(8,128)S(1)} %copy-done.1), custom_call_target="tpu_custom_call" | custom-call | flops 3932160 | bytes 1572864 | tf_op jit(solution)/shard_map/y_inner/pallas_call | solution.py:365
  50.3 1.3 %collective-permute-done.from_right = f32[6,2,8,256]{3,2,1,0:T(8,128)S(1)} collective-permute-done((f32[6,2,8,256]{3,2,1,0:T(8,128)S(1)}, f32[6,2,8,256]{3,2,1,0:T(8,128)S(1)}, u32[]{:S(2)}, u32[]{:S(2)}) %collective-permute-start) | collective-permute-done | bytes 98336 | tf_op jit(solution)/shard_map/ppermute | solution.py:402
  51.5 2.7 %collective-permute-done.1.from_left = f32[6,2,8,256]{3,2,1,0:T(8,128)S(1)} collective-permute-done((f32[6,2,8,256]{3,2,1,0:T(8,128)S(1)}, f32[6,2,8,256]{3,2,1,0:T(8,128)S(1)}, u32[]{:S(2)}, u32[]{:S(2)}) %collective-permute-start.1) | collective-permute-done | bytes 98336 | tf_op jit(solution)/shard_map/ppermute | solution.py:401
  54.2 1.0 %y_edge.1 = f32[6,16,8,256]{3,2,1,0:T(8,128)} custom-call(f32[6,16,8,256]{3,2,1,0:T(8,128)S(1)} %get-tuple-element.8.lattice, f32[6,2,8,256]{3,2,1,0:T(8,128)S(1)} %collective-permute-done.from_right, f32[6,2,8,256]{3,2,1,0:T(8,128)S(1)} %collective-permute-done.1.from_left, s32[16,8,256]{2,1,0:T(8,128)S(1)} %copy-done, ...), custom_call_target="tpu_custom_call", output_to_operand_aliasing={{}: (5, {})} | custom-call | tf_op jit(solution)/shard_map/y_edge/pallas_call | solution.py:381
Async XLA Ops:
  40.7 7.6 %copy-start = (s32[16,8,256]{2,1,0:T(8,128)S(1)}, s32[16,8,256]{2,1,0:T(8,128)}, u32[]{:S(2)}) copy-start(s32[16,8,256]{2,1,0:T(8,128)} %y_offset.3) | copy-start | bytes 393220
  40.7 7.6 %copy-start.1 = (f32[16,8,256]{2,1,0:T(8,128)S(1)}, f32[16,8,256]{2,1,0:T(8,128)}, u32[]{:S(2)}) copy-start(f32[16,8,256]{2,1,0:T(8,128)} %y_frac.3) | copy-start | bytes 393220
  46.7 4.8 %collective-permute-start = (f32[6,2,8,256]{3,2,1,0:T(8,128)S(1)}, f32[6,2,8,256]{3,2,1,0:T(8,128)S(1)}, u32[]{:S(2)}, u32[]{:S(2)}) collective-permute-start(f32[6,2,8,256]{3,2,1,0:T(8,128)S(1)} %get-tuple-element.9), channel_id=1, source_target_pairs={{0,248},{8,0},{16,8},{24,16},{32,24},{40,32},{48,40},{56,48},{64,5... | collective-permute-start | bytes 294920 | tf_op jit(solution)/shard_map/ppermute | solution.py:402
  47.4 6.8 %collective-permute-start.1 = (f32[6,2,8,256]{3,2,1,0:T(8,128)S(1)}, f32[6,2,8,256]{3,2,1,0:T(8,128)S(1)}, u32[]{:S(2)}, u32[]{:S(2)}) collective-permute-start(f32[6,2,8,256]{3,2,1,0:T(8,128)S(1)} %get-tuple-element.10), channel_id=1, source_target_pairs={{0,8},{8,16},{16,24},{24,32},{32,40},{40,48},{48,56},{56,64},{64,7... | collective-permute-start | bytes 294920 | tf_op jit(solution)/shard_map/ppermute | solution.py:401
